TPU v7x, 32 devices: a whole 2x2x4 slice. The times are simulated.
32 devices in a mesh: wide: 16 (over z, y, core), narrow: 2 (over x).
Axes of the slice: x: 2, y: 2, z: 4, core: 2. Of those that a mesh axis runs over, the one named last changes fastest.
Arguments:
- pixels: bfloat16 [2, 32, 272, 261], P(None, ('wide', 'narrow')), may hold values from -4 to 4
- labels: int32 [2, 32], P(None, ('wide', 'narrow')), may hold values from 0 to 999
- partner: int32 [2, 32], P(None, ('wide', 'narrow')), may hold values from 0 to 31
- pair_on: int32 [2, 32], P(None, ('wide', 'narrow')), may hold values 0 or 1
- step_count: int32 [1], replicated, may hold values from 1 to 20
- matrices: float32 [1024, 10240], P(('wide', 'narrow')), may hold values from -0.75 to 0.75, as said below
- kv_weight: float32 [2048, 261], P(('wide', 'narrow')), may hold values from -0.375 to 0.375
- norm_gains: float32 [1024, 10], P(('wide', 'narrow')), may hold values from -1.2 to 1.4, as said below
- head_weight: float32 [1024, 1000], P(('wide', 'narrow')), may hold values from -0.1875 to 0.1875
- latent_init: float32 [1024, 512], P(('wide', 'narrow')), may hold values from -5 to 5
- matrices_first: float32 [1024, 10240], P(('wide', 'narrow')), may hold values from -3.8146973e-05 to 3.8146973e-05
- kv_first: float32 [2048, 261], P(('wide', 'narrow')), may hold values from -3.8146973e-05 to 3.8146973e-05
- gains_first: float32 [1024, 10], P(('wide', 'narrow')), may hold values from -3.8146973e-05 to 3.8146973e-05
- head_first: float32 [1024, 1000], P(('wide', 'narrow')), may hold values from -3.8146973e-05 to 3.8146973e-05
- latent_first: float32 [1024, 512], P(('wide', 'narrow')), may hold values from -8.34465e-07 to 8.34465e-07
- matrices_second: float32 [1024, 10240], P(('wide', 'narrow')), may hold values from 7.949873e-12 to 3.1799494e-11
- kv_second: float32 [2048, 261], P(('wide', 'narrow')), may hold values from 7.949873e-12 to 3.1799494e-11
- gains_second: float32 [1024, 10], P(('wide', 'narrow')), may hold values from 7.949873e-12 to 3.1799494e-11
- head_second: float32 [1024, 1000], P(('wide', 'narrow')), may hold values from 7.949873e-12 to 3.1799494e-11
- latent_second: float32 [1024, 512], P(('wide', 'narrow')), may hold values from 1.5899748e-15 to 6.359899e-15
Outputs:
- total_loss: float32 [], replicated
- grad_norm: float32 [], replicated
- counts: int32 [2], replicated
- new_matrices_first: float32 [1024, 10240], P(('wide', 'narrow'))
- new_matrices_second: float32 [1024, 10240], P(('wide', 'narrow'))
- new_matrices: float32 [1024, 10240], P(('wide', 'narrow'))
- new_kv_first: float32 [2048, 261], P(('wide', 'narrow'))
- new_kv_second: float32 [2048, 261], P(('wide', 'narrow'))
- new_kv_weight: float32 [2048, 261], P(('wide', 'narrow'))
- new_gains_first: float32 [1024, 10], P(('wide', 'narrow'))
- new_gains_second: float32 [1024, 10], P(('wide', 'narrow'))
- clipped_gains: float32 [1024, 10], P(('wide', 'narrow'))
- new_head_first: float32 [1024, 1000], P(('wide', 'narrow'))
- new_head_second: float32 [1024, 1000], P(('wide', 'narrow'))
- new_head_weight: float32 [1024, 1000], P(('wide', 'narrow'))
- new_latent_first: float32 [1024, 512], P(('wide', 'narrow'))
- new_latent_second: float32 [1024, 512], P(('wide', 'narrow'))
- clipped_latent: float32 [1024, 512], P(('wide', 'narrow'))
Inputs may be any that keep to these rules, and one draw needn't show every extreme that they name: `matrices`: the cross and latent output blocks (1 and 7) are four times larger than the others. `norm_gains`: even columns are gains, odd columns biases.
All inputs are finite; a program needn't handle non-finite values. No bound on the sum of `pair_on` on one device may be relied on, other than what follows from the above.
Results may differ from a plain program's by a relative error of at most 0.012.
The roundings to bfloat16 on the way count: a program that leaves them out, or rounds other values in their place, can miss the bound.
Values may be sent and summed in bfloat16 or wider, within the bound.
No kernel may reach another device: no remote copies, remote signals or barrier semaphores. Data moves between devices by JAX's collectives and lax.ppermute only.
A program may use at most 320 MiB of HBM per device.

v0:
```python
import functools

import jax
import jax.numpy as jnp
from jax import lax
from jax.experimental import pallas as pl
from jax.experimental.pallas import tpu as pltpu
from jax.sharding import PartitionSpec as P

HEADS = 8
GROUP = 4
BACK_GROUP = 2
STEPS = 2
FORWARD_STEPS = 1
AXES = ("wide", "narrow")

EPSILON = 1e-05
RATE = 0.03
DECAY = 0.1
TINY = 1e-08
THRESH = 0.01
BEND = 0.044715
MARKS = 128
SLOPE = 0.7978845608028654
VMEM = pltpu.VMEM
MIB = 1 << 20
BIG = 48
PACE = 0.5


def lowered(values):
    return values.astype(jnp.bfloat16)


def dot_nn(first_op, second_op):
    return jnp.dot(first_op, second_op, preferred_element_type=jnp.float32)


def dot_tn(first_op, second_op):
    return lax.dot_general(
        first_op, second_op, (((0,), (0,)), ((), ())), preferred_element_type=jnp.float32
    )


def dot_nt(first_op, second_op):
    return lax.dot_general(
        first_op, second_op, (((1,), (1,)), ((), ())), preferred_element_type=jnp.float32
    )


def standard(inputs):
    center = inputs - jnp.mean(inputs, axis=-1, keepdims=True)
    scale = lax.rsqrt(jnp.mean(center * center, axis=-1, keepdims=True) + EPSILON)
    return center * scale, scale


def layer_norm(inputs, scales, column):
    return standard(inputs)[0] * scales[column : column + 1, :] + scales[column + 1 : column + 2, :]


def norm_back(inputs, scales, column, upstream):
    unit, scale = standard(inputs)
    gain = jnp.sum(upstream * unit, axis=0, keepdims=True)
    bias = jnp.sum(upstream, axis=0, keepdims=True)
    inner = upstream * scales[column : column + 1, :]
    back = scale * (
        inner
        - jnp.mean(inner, axis=-1, keepdims=True)
        - unit * jnp.mean(inner * unit, axis=-1, keepdims=True)
    )
    return back, gain, bias


def gelu_both(values):
    square = values * values
    bent = jnp.tanh(SLOPE * values * (1.0 + BEND * square))
    half = 0.5 * (1.0 + bent)
    steep = half + 0.5 * values * (1.0 - bent * bent) * SLOPE * (1.0 + 3.0 * BEND * square)
    return values * half, steep


def softmax(scores):
    raised = jnp.exp(scores - jnp.max(scores, axis=-1, keepdims=True))
    return raised * (1.0 / jnp.sum(raised, axis=-1, keepdims=True))


def softmax_back(attend, upstream):
    return attend * (upstream - jnp.sum(upstream * attend, axis=-1, keepdims=True))


class Half:
    def __init__(self, arrays, offsets, rows):
        self.arrays = arrays
        self.offsets = offsets
        self.rows = rows

    def start(self, refs, me, target, sem, column, stride=None, shift=0):
        width = target.shape[1]
        if self.offsets is None:
            pltpu.make_async_copy(refs[0].at[0, :, column : column + width], target, sem).start()
            return
        stride = self.rows if stride is None else stride
        for ref, offsets in zip(refs, self.offsets):
            for group, offset in enumerate(offsets):
                spot = pl.multiple_of((me ^ offset) * stride + shift, self.rows)
                pltpu.make_async_copy(
                    ref.at[group, :, column : column + width],
                    target.at[pl.ds(spot, self.rows), :],
                    sem,
                ).start()


class Joint:
    def __init__(self, pieces):
        self.pieces = pieces
        self.arrays = [array for half, *_ in pieces for array in half.arrays]

    def start(self, refs, me, target, sem, column):
        at = 0
        for half, spot, first, last in self.pieces:
            count = len(half.arrays)
            half.start(refs[at : at + count], me, target.at[:, first:last], sem, spot)
            at += count


def arrived(target, sem):
    pltpu.make_async_copy(target, target, sem).wait()


def cost(micros):
    return pl.CostEstimate(flops=int(micros * PACE * 1.1e9), bytes_accessed=1 << 10, transcendentals=0)


def params(mib, dims=1, big=None):
    return pltpu.CompilerParams(
        vmem_limit_bytes=(big or max(mib, BIG)) * MIB, dimension_semantics=("arbitrary",) * dims
    )


def launch(kernel, after, operands, in_specs, **rest):
    extra = len(after)

    def inner(*refs):
        kernel(*refs[: len(operands)], *refs[len(operands) + extra :])

    return pl.pallas_call(inner, in_specs=list(in_specs) + [ANY] * extra, **rest)(*operands, *after)


ANY = pl.BlockSpec(memory_space=pl.ANY)
SMEM = pl.BlockSpec(memory_space=pltpu.SMEM)


def whole(shape):
    return pl.BlockSpec(shape, lambda *ids: (0,) * len(shape))


def by_crop(shape, rank=1):
    return pl.BlockSpec(shape, lambda m, *ids: (m,) + (0,) * (len(shape) - 1))


def shaped(shape, dtype):
    return jax.ShapeDtypeStruct(shape, dtype)


def run_cross_forward(me, pictures, small, kv, first, second, width, tokens, after=()):
    micro, spots, channels = pictures.shape
    parts = (small, kv, first, second)
    counts = [len(part[0].arrays) for part in parts]
    small_columns = tokens + 128

    def kernel(me_ref, pic_ref, *refs):
        groups = []
        at = 0
        for count in counts:
            groups.append(refs[at : at + count])
            at += count
        latent_ref, blended_ref, attend_ref, pair_ref, initial_ref, hidden_ref, query_ref, scale_ref = refs[at : at + 8]
        small_s, kv_s, first_s, second_s, sems = refs[at + 8 :]
        me_now = me_ref[0]
        step = pl.program_id(0)

        @pl.when(step == 0)
        def _():
            small[0].start(groups[0], me_now, small_s, sems.at[0], small[1])
            if kv[0].offsets is None:
                kv[0].start(groups[1], me_now, kv_s, sems.at[1], 0)
            else:
                rows = kv[0].rows
                kv[0].start(groups[1], me_now, kv_s, sems.at[1], kv[1], 2 * rows, 0)
                kv[0].start(groups[1], me_now, kv_s, sems.at[1], kv[1] + channels, 2 * rows, rows)
            first[0].start(groups[2], me_now, first_s, sems.at[2], first[1])
            second[0].start(groups[3], me_now, second_s, sems.at[3], second[1])
            arrived(small_s, sems.at[0])
            turned = small_s[...].astype(jnp.float32).T
            initial_ref[...] = turned[:tokens]
            scale_ref[...] = turned[tokens : tokens + 16]
            hidden_ref[...] = lowered(layer_norm(initial_ref[...], scale_ref, 0))
            arrived(first_s, sems.at[2])
            query_ref[...] = lowered(dot_nn(hidden_ref[...], first_s[...]))
            arrived(kv_s, sems.at[1])
            arrived(second_s, sems.at[3])

        pair_ref[0] = lowered(dot_nt(pic_ref[0], kv_s[...]))
        scores = dot_nt(query_ref[...], pair_ref[0, :, :width]) * width ** (-0.5)
        attend = softmax(scores)
        attend_ref[0] = attend
        blended_ref[...] = lowered(dot_nn(lowered(attend), pair_ref[0, :, width:]))
        latent_ref[...] = initial_ref[...] + dot_nn(blended_ref[...], second_s[...])

    total = micro * tokens
    return launch(
        kernel,
        after,
        [me, pictures, *[array for part in parts for array in part[0].arrays]],
        grid=(micro,),
        in_specs=[SMEM, by_crop((1, spots, channels))] + [ANY] * sum(counts),
        out_specs=[
            by_crop((tokens, width)),
            by_crop((tokens, width)),
            by_crop((1, tokens, spots)),
            by_crop((1, spots, 2 * width)),
            whole((tokens, width)),
            whole((tokens, width)),
            whole((tokens, width)),
            whole((16, width)),
        ],
        out_shape=[
            shaped((total, width), jnp.float32),
            shaped((total, width), jnp.bfloat16),
            shaped((micro, tokens, spots), jnp.float32),
            shaped((micro, spots, 2 * width), jnp.bfloat16),
            shaped((tokens, width), jnp.float32),
            shaped((tokens, width), jnp.bfloat16),
            shaped((tokens, width), jnp.bfloat16),
            shaped((16, width), jnp.float32),
        ],
        scratch_shapes=[
            VMEM((width, small_columns), jnp.bfloat16),
            VMEM((2 * width, channels), jnp.bfloat16),
            VMEM((width, width), jnp.bfloat16),
            VMEM((width, width), jnp.bfloat16),
            pltpu.SemaphoreType.DMA((4,)),
        ],
        compiler_params=params(48),
        cost_estimate=cost(18),
        name="cross_forward",
    )


def run_feed_forward(me, scales, latent, first, second, column, micro, pool, prior=None, after=()):
    total, width = latent.shape
    tokens = total // micro
    rows = tokens // FORWARD_STEPS
    parts = [first, second] + ([prior[1]] if prior else [])
    counts = [len(part[0].arrays) for part in parts]

    def kernel(me_ref, scale_ref, latent_ref, *refs):
        if prior:
            prior_refs, refs = refs[:micro], refs[micro:]
        groups = []
        at = 0
        for count in counts:
            groups.append(refs[at : at + count])
            at += count
        out_ref, hidden_ref, active_ref, steep_ref = refs[at : at + 4]
        more = refs[at + 4 : -2 - len(parts)]
        blocks, pool_s, sems = refs[-2 - len(parts) : -2], refs[-2], refs[-1]
        first_s, second_s = blocks[:2]
        step = pl.program_id(0)

        @pl.when(step == 0)
        def _():
            for number in range(len(parts) - 1, -1, -1) if prior else range(len(parts)):
                parts[number][0].start(
                    groups[number], me_ref[0], blocks[number], sems.at[number], parts[number][1]
                )

        source_ref = latent_ref
        if prior:
            source_ref = more[-1]

            @pl.when(step == 0)
            def _():
                arrived(blocks[2], sems.at[2])

            for number in range(micro * FORWARD_STEPS):

                @pl.when(step == number)
                def _():
                    first_row = (number % FORWARD_STEPS) * rows
                    source_ref[...] = latent_ref[...] + dot_nn(
                        prior_refs[number // FORWARD_STEPS][first_row : first_row + rows, :], blocks[2][...]
                    )

        hidden_ref[...] = lowered(layer_norm(source_ref[...], scale_ref, column))

        @pl.when(step == 0)
        def _():
            arrived(first_s, sems.at[0])

        pieces = 4
        span = width // pieces
        for piece in range(pieces):
            cut = slice(piece * span, (piece + 1) * span)
            active, steep = gelu_both(dot_nn(hidden_ref[...], first_s[:, cut]))
            active_ref[:, cut] = lowered(active)
            steep_ref[:, cut] = lowered(steep)

        @pl.when(step == 0)
        def _():
            arrived(second_s, sems.at[1])

        out_ref[...] = source_ref[...] + dot_nn(active_ref[...], second_s[...])
        if pool:
            normed = layer_norm(out_ref[...], scale_ref, 8)
            part = jnp.sum(normed, axis=0, keepdims=True)

            @pl.when(step % FORWARD_STEPS == 0)
            def _():
                pool_s[...] = part

            @pl.when(step % FORWARD_STEPS != 0)
            def _():
                pool_s[...] += part

            @pl.when(step % FORWARD_STEPS == FORWARD_STEPS - 1)
            def _():
                more[0][0] = lowered(pool_s[...] / tokens)

    out_shape = [shaped((total, width), jnp.float32)] + [shaped((total, width), jnp.bfloat16)] * 3
    out_specs = [by_crop((rows, width))] * 4
    if pool:
        out_shape.append(shaped((micro, 1, width), jnp.bfloat16))
        out_specs.append(pl.BlockSpec((1, 1, width), lambda m: (m // FORWARD_STEPS, 0, 0)))
    in_specs = [SMEM, whole((16, width)), by_crop((rows, width))]
    operands = [me, scales, latent]
    if prior:
        out_shape.append(shaped((total, width), jnp.float32))
        out_specs.append(by_crop((rows, width)))
        in_specs += [whole((tokens, width))] * micro
        operands += prior[0]
    return launch(
        kernel,
        after,
        operands + [array for part in parts for array in part[0].arrays],
        in_specs + [ANY] * sum(counts),
        grid=(micro * FORWARD_STEPS,),
        out_specs=out_specs,
        out_shape=out_shape,
        scratch_shapes=[VMEM((width, width), jnp.bfloat16)] * len(parts)
        + [VMEM((1, width), jnp.float32), pltpu.SemaphoreType.DMA((len(parts),))],
        compiler_params=params(48, big=60),
        cost_estimate=cost(18),
        name="feed_forward",
    )


def run_self_forward(crop, me, scales, latent, query, key, value, micro, after=()):
    total, width = latent.shape
    tokens = total // micro
    part = width // HEADS
    pair = GROUP * part
    turns = HEADS // GROUP
    parts = (query, key, value)
    counts = [len(entry[0].arrays) for entry in parts]

    def kernel(me_ref, scale_ref, latent_ref, *refs):
        groups = []
        at = 0
        for count in counts:
            groups.append(refs[at : at + count])
            at += count
        hidden_ref, packed_ref, attend_ref, blended_ref, packed_s, sems = refs[at:]
        turn = pl.program_id(0)

        @pl.when(turn == 0)
        def _():
            for number in range(3):
                parts[number][0].start(
                    groups[number], me_ref[0], packed_s.at[number], sems.at[number], parts[number][1]
                )
            hidden_ref[...] = lowered(layer_norm(latent_ref[...], scale_ref, 4))
            for number in range(3):
                arrived(packed_s.at[number], sems.at[number])
                packed_ref[:, number * width : (number + 1) * width] = lowered(
                    dot_nn(hidden_ref[...], packed_s[number])
                )

        base = pl.multiple_of(turn * pair, pair)
        queries = packed_ref[:, pl.ds(base, pair)]
        keys = packed_ref[:, pl.ds(pl.multiple_of(width + base, pair), pair)]
        values = packed_ref[:, pl.ds(pl.multiple_of(2 * width + base, pair), pair)]
        joined = []
        for head in range(GROUP):
            cut = slice(head * part, (head + 1) * part)
            attend = lowered(softmax(dot_nt(queries[:, cut], keys[:, cut]) * part ** (-0.5)))
            attend_ref[head] = attend
            joined.append(lowered(dot_nn(attend, values[:, cut])))
        blended_ref[:, pl.ds(base, pair)] = jnp.concatenate(joined, axis=1)

    return launch(
        kernel,
        after,
        [me, scales, latent, *[array for entry in parts for array in entry[0].arrays]],
        [
            SMEM,
            whole((16, width)),
            pl.BlockSpec((tokens, width), lambda h: (crop, 0)),
        ]
        + [ANY] * sum(counts),
        grid=(turns,),
        out_specs=[
            whole((tokens, width)),
            whole((tokens, 3 * width)),
            pl.BlockSpec((GROUP, tokens, tokens), lambda h: (h, 0, 0)),
            whole((tokens, width)),
        ],
        out_shape=[
            shaped((tokens, width), jnp.bfloat16),
            shaped((tokens, 3 * width), jnp.bfloat16),
            shaped((HEADS, tokens, tokens), jnp.bfloat16),
            shaped((tokens, width), jnp.bfloat16),
        ],
        scratch_shapes=[
            VMEM((3, width, width), jnp.bfloat16),
            pltpu.SemaphoreType.DMA((3,)),
        ],
        compiler_params=params(48, big=60),
        cost_estimate=cost(14),
        name="self_forward",
    )


def run_losses(me, pooled, head, classes, examples, micro, after=()):
    count, width = pooled.shape[0], pooled.shape[1] - MARKS
    parts = (head[0], head[1])
    counts = [len(entry[0].arrays) for entry in parts]
    span = width // 2

    def kernel(me_ref, pooled_ref, *refs):
        groups = (refs[: counts[0]], refs[counts[0] : counts[0] + counts[1]])
        loss_ref, logits_ref, grad_ref, left_s, right_s, sems = refs[counts[0] + counts[1] :]
        me_now = me_ref[0]
        halves = (left_s, right_s)
        for number in range(2):
            parts[number][0].start(
                groups[number], me_now, halves[number], sems.at[number], parts[number][1]
            )
        rows = lax.broadcasted_iota(jnp.int32, (count, 1), 0)
        turn = rows % micro
        marks = pooled_ref[:, width:].astype(jnp.float32)
        labels = (marks[:, 0:1] * 256.0 + marks[:, 1:2]).astype(jnp.int32)
        partner = (marks[:, 2:3] * 256.0 + marks[:, 3:4]).astype(jnp.int32)
        active = marks[:, 4:5]
        pooled_low = pooled_ref[:, :width]
        pooled_wide = pooled_low.astype(jnp.float32)
        columns = lax.broadcasted_iota(jnp.int32, (count, count), 1)
        aimed = lowered((columns == partner * micro + turn).astype(jnp.float32))
        distance = pooled_wide - dot_nn(aimed, pooled_low)
        divisor = jnp.zeros((count, 1), jnp.float32)
        for number in range(micro):
            here = (turn == number).astype(jnp.float32)
            counted = jnp.sum(here * active, axis=0, keepdims=True)
            loss_ref[1 + number : 2 + number] = jnp.broadcast_to(counted, (1, 128))
            counted = jnp.maximum(counted, 1.0)
            divisor = divisor + here * (counted * width**0.5)
        agreement = active * jnp.sum(distance * distance, axis=-1, keepdims=True) / divisor
        pull = (2.0 / micro) * (active / divisor) * distance
        for number in range(2):
            arrived(halves[number], sems.at[number])
        logits = jnp.concatenate([dot_nn(pooled_low, half[...]) for half in halves], axis=1)
        column = lax.broadcasted_iota(jnp.int32, (count, 2 * span), 1)
        logits = jnp.where(column < classes, logits, -1e30)
        top = jnp.max(logits, axis=-1, keepdims=True)
        raised = jnp.exp(logits - top)
        mass = jnp.sum(raised, axis=-1, keepdims=True)
        hot = (column == labels).astype(jnp.float32)
        entropy = top + jnp.log(mass) - jnp.sum(logits * hot, axis=-1, keepdims=True)
        loss = jnp.sum(entropy / examples + agreement, axis=0, keepdims=True) / micro
        loss_ref[0:1] = jnp.broadcast_to(loss, (1, 128))
        grad_logits = lowered((raised / mass - hot) / (examples * micro))
        logits_ref[...] = grad_logits
        grad = pull + sum(
            dot_nt(grad_logits[:, number * span : (number + 1) * span], halves[number][...])
            for number in range(2)
        )
        for number in range(micro):
            own = (rows == me_now * micro + number).astype(jnp.float32)
            aiming = ((partner == me_now) & (turn == number)).astype(jnp.float32)
            grad_ref[number] = jnp.sum(own * grad - aiming * pull, axis=0, keepdims=True)

    return launch(
        kernel,
        after,
        [me, pooled, *[array for entry in parts for array in entry[0].arrays]],
        in_specs=[SMEM, whole(pooled.shape)] + [ANY] * sum(counts),
        grid=(1,),
        out_specs=[whole((8, 128)), whole((count, width)), whole((micro, 1, width))],
        out_shape=[
            shaped((8, 128), jnp.float32),
            shaped((count, width), jnp.bfloat16),
            shaped((micro, 1, width), jnp.float32),
        ],
        scratch_shapes=[
            VMEM((width, span), jnp.bfloat16),
            VMEM((width, span), jnp.bfloat16),
            pltpu.SemaphoreType.DMA((2,)),
        ],
        compiler_params=pltpu.CompilerParams(vmem_limit_bytes=24 * MIB),
        cost_estimate=cost(5),
        name="losses",
    )


class Sender:
    def __init__(self, total, core_rows):
        self.total = total
        self.core_rows = core_rows
        self.groups = total // (2 * core_rows)

    def shapes(self, columns):
        return [shaped((self.groups, self.core_rows, columns), jnp.bfloat16)] * 2

    def start(self, source, core, keep, send, column, sem):
        width = source.shape[1]
        rows = self.core_rows
        for group in range(self.groups):
            for target, side in ((send, 1 - core), (keep, core)):
                spot = pl.multiple_of((2 * group + side) * rows, rows)
                pltpu.make_async_copy(
                    source.at[pl.ds(spot, rows), :],
                    target.at[group, :, column : column + width],
                    sem,
                ).start()


    def start_rows(self, source, core, keep, send, column, rows, side, sem):
        width = source.shape[1]
        each = self.core_rows // rows
        for group in range(self.groups):
            for target, half in ((send, 1 - core), (keep, core)):
                for device in range(each):
                    first = ((2 * group + half) * each + device) * 2 * rows + side * rows
                    pltpu.make_async_copy(
                        source.at[pl.ds(pl.multiple_of(first, rows), rows), :],
                        target.at[group, device * rows : (device + 1) * rows, column : column + width],
                        sem,
                    ).start()


def run_feed_backward(
    me, scales, latent, upstream, steep, first, second, column, micro, pool, crop=None, after=()
):
    total, width = latent.shape
    tokens = total // micro
    rows = tokens // STEPS
    parts = (first, second)
    counts = [len(entry[0].arrays) for entry in parts]
    span = width // 2

    def kernel(me_ref, scale_ref, latent_ref, up_ref, *refs):
        if pool:
            pooled_ref, refs = refs[0], refs[1:]
        steep_ref, refs = refs[0], refs[1:]
        first_refs, refs = refs[: counts[0]], refs[counts[0] :]
        second_refs, refs = refs[: counts[1]], refs[counts[1] :]
        out_ref, gain_ref, low_ref, before_ref, after_ref, first_s, second_s, sems = refs
        step = pl.program_id(0)

        @pl.when(step == 0)
        def _():
            second[0].start(second_refs, me_ref[0], second_s, sems.at[1], second[1])
            first[0].start(first_refs, me_ref[0], first_s, sems.at[0], first[1])
            gain_ref[...] = jnp.zeros(gain_ref.shape, jnp.float32)

        if pool:
            spread = jnp.broadcast_to(pooled_ref[0] / tokens, (rows, width))
            upstream, gain, bias = norm_back(up_ref[...], scale_ref, 8, spread)
            gain_ref[2:3] += gain
            gain_ref[3:4] += bias
            out_ref[...] = upstream
        else:
            out_ref[...] = up_ref[...]
        low_ref[...] = lowered(out_ref[...])

        @pl.when(step == 0)
        def _():
            arrived(second_s, sems.at[1])

        for number in range(2):
            cut = slice(number * span, (number + 1) * span)
            grad = dot_nt(low_ref[...], second_s[cut, :])
            before_ref[:, cut] = lowered(grad * steep_ref[:, cut].astype(jnp.float32))

        @pl.when(step == 0)
        def _():
            arrived(first_s, sems.at[0])

        back, gain, bias = norm_back(
            latent_ref[...], scale_ref, column, dot_nt(before_ref[...], first_s[...])
        )
        gain_ref[0:1] += gain
        gain_ref[1:2] += bias
        out_ref[...] += back
        after_ref[...] = lowered(out_ref[...])

    rows_of = by_crop((rows, width))
    if crop is not None:
        rows_of = pl.BlockSpec((rows, width), lambda m: (crop * STEPS + m, 0))
        total = tokens
    in_specs = [SMEM, whole((16, width)), rows_of, rows_of]
    operands = [me, scales, latent]
    if pool:
        in_specs.append(pl.BlockSpec((1, 1, width), lambda m: (m // STEPS, 0, 0)))
        operands += list(upstream)
    else:
        operands.append(upstream)
    in_specs += [rows_of] + [ANY] * sum(counts)
    operands += [steep] + [array for entry in parts for array in entry[0].arrays]
    return launch(
        kernel,
        after,
        operands,
        in_specs,
        grid=(micro * STEPS if crop is None else STEPS,),
        out_specs=[by_crop((rows, width)), whole((8, width))] + [by_crop((rows, width))] * 3,
        out_shape=[shaped((total, width), jnp.float32), shaped((8, width), jnp.float32)]
        + [shaped((total, width), jnp.bfloat16)] * 3,
        scratch_shapes=[
            VMEM((width, width), jnp.bfloat16),
            VMEM((width, width), jnp.bfloat16),
            pltpu.SemaphoreType.DMA((2,)),
        ],
        compiler_params=params(48, big=60),
        cost_estimate=cost(16 if crop is None else 9),
        name="feed_backward",
    )


def run_self_backward(crop, me, scales, latent, upstream, stored, query, key, value, out, micro, onward, after=()):
    total, width = latent.shape
    tokens = total // micro
    part = width // HEADS
    pair = BACK_GROUP * part
    turns = HEADS // BACK_GROUP
    packed, attend = stored
    parts = (query, key, value, out)
    counts = [len(entry[0].arrays) for entry in parts]

    def kernel(me_ref, scale_ref, latent_ref, up_ref, packed_any, attend_ref, *refs):
        groups = []
        at = 0
        for count in counts:
            groups.append(refs[at : at + count])
            at += count
        if onward is not None:
            at += 1
        grad_out, out_ref, gain_ref, packed_s, out_s, blend_s, grad_ref, latent_s, packed_ref, sems = (
            refs[at:]
        )
        turn = pl.program_id(0)

        @pl.when(turn == 0)
        def _():
            out[0].start(groups[3], me_ref[0], out_s, sems.at[3], out[1])
            pltpu.make_async_copy(packed_any, packed_ref, sems.at[6]).start()
            for number in range(3):
                parts[number][0].start(
                    groups[number], me_ref[0], packed_s.at[number], sems.at[number], parts[number][1]
                )
            pltpu.make_async_copy(
                latent_ref.at[crop * tokens : (crop + 1) * tokens, :], latent_s, sems.at[4]
            ).start()
            arrived(out_s, sems.at[3])
            blend_s[...] = lowered(dot_nt(lowered(up_ref[...]), out_s[...]))
            arrived(packed_ref, sems.at[6])

        base = pl.multiple_of(turn * pair, pair)
        queries = packed_ref[:, pl.ds(base, pair)]
        keys = packed_ref[:, pl.ds(pl.multiple_of(width + base, pair), pair)]
        values = packed_ref[:, pl.ds(pl.multiple_of(2 * width + base, pair), pair)]
        blends = blend_s[:, pl.ds(base, pair)]
        grads = ([], [], [])
        for head in range(BACK_GROUP):
            cut = slice(head * part, (head + 1) * part)
            attend = attend_ref[head]
            grad_attend = dot_nt(blends[:, cut], values[:, cut])
            scores = lowered(
                softmax_back(attend.astype(jnp.float32), grad_attend) * part ** (-0.5)
            )
            grads[2].append(lowered(dot_tn(attend, blends[:, cut])))
            grads[0].append(lowered(dot_nn(scores, keys[:, cut])))
            grads[1].append(lowered(dot_tn(scores, queries[:, cut])))
        for number in range(3):
            spot = pl.ds(pl.multiple_of(number * width + base, pair), pair)
            grad_ref[:, spot] = jnp.concatenate(grads[number], axis=1)
            pltpu.make_async_copy(grad_ref.at[:, spot], grad_out.at[:, spot], sems.at[5]).start()

        @pl.when(turn == turns - 1)
        def _():
            for number in range(3):
                arrived(packed_s.at[number], sems.at[number])
            grad_hidden = sum(
                dot_nt(grad_ref[:, number * width : (number + 1) * width], packed_s[number])
                for number in range(3)
            )
            arrived(latent_s, sems.at[4])
            back, gain, bias = norm_back(latent_s[...], scale_ref, 4, grad_hidden)
            gain_ref[0:1] = gain
            gain_ref[1:2] = bias
            out_ref[...] = up_ref[...] + back
            arrived(grad_ref, sems.at[5])

    def crop_rows(columns):
        return pl.BlockSpec((tokens, columns), lambda h: (crop, 0))

    operands = [me, scales, latent, upstream, packed, attend]
    operands += [array for entry in parts for array in entry[0].arrays]
    aliases = {}
    if onward is not None:
        aliases = {len(operands): 1}
        operands.append(onward)
    return launch(
        kernel,
        after,
        operands,
        grid=(turns,),
        in_specs=[
            SMEM,
            whole((16, width)),
            ANY,
            crop_rows(width),
            ANY,
            pl.BlockSpec((BACK_GROUP, tokens, tokens), lambda h: (h, 0, 0)),
        ]
        + [ANY] * (sum(counts) + len(aliases)),
        input_output_aliases=aliases,
        out_specs=[ANY, crop_rows(width), whole((8, width))],
        out_shape=[
            shaped((tokens, 3 * width), jnp.bfloat16),
            shaped((total, width), jnp.float32),
            shaped((8, width), jnp.float32),
        ],
        scratch_shapes=[
            VMEM((3, width, width), jnp.bfloat16),
            VMEM((width, width), jnp.bfloat16),
            VMEM((tokens, width), jnp.bfloat16),
            VMEM((tokens, 3 * width), jnp.bfloat16),
            VMEM((tokens, width), jnp.float32),
            VMEM((tokens, 3 * width), jnp.bfloat16),
            pltpu.SemaphoreType.DMA((7,)),
        ],
        compiler_params=params(56),
        cost_estimate=cost(20),
        name="self_backward",
    )


def run_weights(me, products, sender, after=()):
    flat = []
    for lefts, rights in products:
        for array, *_ in lefts + rights:
            if not any(array is known for known in flat):
                flat.append(array)
    where = {id(array): number for number, array in enumerate(flat)}
    width = products[0][0][0][0].shape[1]
    count = len(products)
    span = width // 2

    def kernel(me_ref, *refs):
        sources, (keep, send, mat_s), sems = refs[: len(flat)], refs[len(flat) : len(flat) + 3], refs[-1]
        held = refs[len(flat) + 3 : -1]
        core = (me_ref[0] // me_ref[1]) % 2
        copies = [
            pltpu.make_async_copy(source, target, sems.at[1 + number])
            for number, (source, target) in enumerate(zip(sources, held))
        ]
        for copy in copies:
            copy.start()
        there = set()
        for number, (lefts, rights) in enumerate(products):
            for array, *_ in lefts + rights:
                if where[id(array)] not in there:
                    there.add(where[id(array)])
                    copies[where[id(array)]].wait()
            for side in range(2):
                cut = slice(side * span, (side + 1) * span)
                mat_s[number, :, cut] = lowered(
                    sum(
                        dot_tn(
                            held[where[id(left)]][begin : begin + size, :],
                            held[where[id(right)]][
                                top : top + size, at + side * span : at + (side + 1) * span
                            ],
                        )
                        for (left, begin, size), (right, top, at) in zip(lefts, rights)
                    )
                )
            sender.start(mat_s.at[number], core, keep, send, number * width, sems.at[0])
        arrived(mat_s, sems.at[0])

    return launch(
        kernel,
        after,
        [me] + flat,
        [SMEM] + [ANY] * len(flat),
        out_specs=[ANY] * 2,
        out_shape=sender.shapes(count * width),
        scratch_shapes=[VMEM((count, width, width), jnp.bfloat16)]
        + [VMEM(array.shape, array.dtype) for array in flat]
        + [pltpu.SemaphoreType.DMA((1 + len(flat),))],
        compiler_params=pltpu.CompilerParams(vmem_limit_bytes=60 * MIB),
        cost_estimate=cost(3 * count),
        name="weights",
    )


def run_cross_backward(
    crop, me, scales, initial, ups, stored, gains, first, second, micro, before, after=()
):
    tokens, width = ups[crop].shape
    queries, attend, pairs = stored
    spots = pairs.shape[1]
    parts = (first, second)
    counts = [len(entry[0].arrays) for entry in parts]
    small_columns = tokens + 128
    last = crop == micro - 1

    def kernel(me_ref, scale_ref, initial_ref, up_ref, query_ref, attend_ref, pair_ref, gains_ref, *refs):
        if before is not None:
            before_ref, refs = refs[0], refs[1:]
        if last:
            others, refs = refs[: micro - 1], refs[micro - 1 :]
        first_refs, refs = refs[: counts[0]], refs[counts[0] :]
        second_refs, refs = refs[: counts[1]], refs[counts[1] :]
        query_out, pair_out, back_ref, first_s, second_s, sems = refs
        second[0].start(second_refs, me_ref[0], second_s, sems.at[1], second[1])
        first[0].start(first_refs, me_ref[0], first_s, sems.at[0], first[1])
        keys, values = pair_ref[0, :, :width], pair_ref[0, :, width:]
        attend = attend_ref[0]
        arrived(second_s, sems.at[1])
        blend = lowered(dot_nt(lowered(up_ref[...]), second_s[...]))
        scores = lowered(softmax_back(attend, dot_nt(blend, values)) * width ** (-0.5))
        query_out[...] = lowered(dot_nn(scores, keys))
        pair_out[:, :width] = lowered(dot_tn(scores, query_ref[...]))
        pair_out[:, width:] = lowered(dot_tn(lowered(attend), blend))
        arrived(first_s, sems.at[0])
        back = dot_nt(query_out[...], first_s[...])
        if before is not None:
            back = before_ref[...] + back
        if not last:
            back_ref[...] = back
            return
        back, gain, bias = norm_back(initial_ref[...], scale_ref, 0, back)
        for other in (up_ref, *others):
            back = back + other[...]
        gains_all = jnp.concatenate(
            [gain, bias, gains_ref[2:, :], jnp.zeros((128 - gains_ref.shape[0], width), jnp.float32)], axis=0
        )
        back_ref[:, :tokens] = lowered(back.T)
        back_ref[:, tokens:] = lowered(gains_all.T)

    back_shape = (
        shaped((width, small_columns), jnp.bfloat16) if last else shaped((tokens, width), jnp.float32)
    )
    extra = [] if before is None else [before]
    if last:
        extra += ups[:crop]
    return launch(
        kernel,
        after,
        [me, scales, initial, ups[crop], queries, attend, pairs, gains]
        + extra
        + [array for entry in parts for array in entry[0].arrays],
        [
            SMEM,
            whole((16, width)),
            whole((tokens, width)),
            whole((tokens, width)),
            whole((tokens, width)),
            pl.BlockSpec((1, tokens, spots), lambda i: (crop, 0, 0)),
            pl.BlockSpec((1, spots, 2 * width), lambda i: (crop, 0, 0)),
            whole((16, width)),
        ]
        + [whole((tokens, width))] * len(extra)
        + [ANY] * sum(counts),
        grid=(1,),
        out_specs=[whole((tokens, width)), whole((spots, 2 * width)), whole(back_shape.shape)],
        out_shape=[
            shaped((tokens, width), jnp.bfloat16),
            shaped((spots, 2 * width), jnp.bfloat16),
            back_shape,
        ],
        scratch_shapes=[
            VMEM((width, width), jnp.bfloat16),
            VMEM((width, width), jnp.bfloat16),
            pltpu.SemaphoreType.DMA((2,)),
        ],
        compiler_params=params(48),
        cost_estimate=cost(9),
        name="cross_backward",
    )


def run_last_weights(me, hidden, grad_queries, grad_pairs, pictures, small, sender, rows, apart, after=()):
    tokens, width = hidden.shape
    micro = len(grad_queries)
    channels = pictures.shape[2]
    small_columns = small.shape[1]
    kv_sender = Sender(2 * width, 2 * sender.core_rows)

    def kernel(me_ref, hidden_ref, *refs):
        query_refs, pair_refs = refs[:micro], refs[micro : 2 * micro]
        pic_ref, small_ref, keep, send = refs[2 * micro : 2 * micro + 4]
        refs = refs[2 * micro + 4 :]
        mat_s, kv_s, sems = refs[-3:]
        core = (me_ref[0] // me_ref[1]) % 2
        sender.start(small_ref, core, keep, send, width, sems.at[2])
        span = width // 2
        for number in range(2):
            cut = slice(number * span, (number + 1) * span)
            mat_s[:, cut] = lowered(
                sum(
                    dot_tn(hidden_ref[...], query_refs[crop][:, cut]) for crop in range(micro)
                )
            )
        sender.start(mat_s, core, keep, send, 0, sems.at[0])
        kv_s[...] = lowered(sum(dot_tn(pair_refs[crop][...], pic_ref[crop]) for crop in range(micro)))
        if apart:
            kv_sender.start(kv_s, core, refs[0], refs[1], 0, sems.at[1])
        else:
            for side in range(2):
                sender.start_rows(
                    kv_s, core, keep, send, width + small_columns + side * channels, rows, side, sems.at[1]
                )
        arrived(mat_s, sems.at[0])
        arrived(kv_s, sems.at[1])
        arrived(small_ref, sems.at[2])

    operands = [me, hidden, *grad_queries, *grad_pairs, pictures, small]
    if apart:
        shapes = sender.shapes(width + small_columns) + kv_sender.shapes(channels)
    else:
        shapes = sender.shapes(width + small_columns + 2 * channels)
    return launch(
        kernel,
        after,
        operands,
        [SMEM] + [whole(array.shape) for array in operands[1:]],
        grid=(1,),
        out_specs=[ANY] * len(shapes),
        out_shape=shapes,
        scratch_shapes=[
            VMEM((width, width), jnp.bfloat16),
            VMEM((2 * width, channels), jnp.bfloat16),
            pltpu.SemaphoreType.DMA((3,)),
        ],
        compiler_params=pltpu.CompilerParams(vmem_limit_bytes=BIG * MIB),
        cost_estimate=cost(6),
        name="last_weights",
    )


def run_shards(matrices, kv_weight, norm_gains, head_weight, latent_init, columns):
    rows = matrices.shape[0]
    tokens, gains = latent_init.shape[1], norm_gains.shape[0]
    channels = kv_weight.shape[1]
    wide_channels = -(-channels // 128) * 128
    classes = head_weight.shape[1]
    width = matrices.shape[1] // 10
    small = tokens + 128

    def kernel(mat_ref, kv_ref, gain_ref, head_ref, latent_ref, first_ref, *refs):
        first_ref[:, tokens:small] = jnp.zeros((rows, small - tokens), jnp.bfloat16)
        first_ref[:, :tokens] = lowered(latent_ref[...])
        first_ref[:, tokens : tokens + gains] = lowered(gain_ref[...].T)
        first_ref[:, small : small + 2 * width] = lowered(mat_ref[:, : 2 * width])
        first_ref[:, small + 2 * width :] = jnp.zeros((rows, 2 * wide_channels), jnp.bfloat16)
        for side in range(2):
            at = small + 2 * width + side * wide_channels
            first_ref[:, at : at + channels] = lowered(kv_ref[side * rows : (side + 1) * rows, :])
        for (begin, end), ref in zip(columns, refs):
            ref[:, : (end - begin) * width] = lowered(mat_ref[:, begin * width : end * width])
        at = refs[-1].shape[1] - width
        refs[-1][:, at:] = jnp.zeros((rows, width), jnp.bfloat16)
        refs[-1][:, at : at + classes] = lowered(head_ref[...])

    widths = [small + 2 * width + 2 * wide_channels] + [(end - begin) * width for begin, end in columns]
    widths[-1] += width
    return pl.pallas_call(
        kernel,
        grid=(1,),
        in_specs=[
            whole(array.shape)
            for array in (matrices, kv_weight, norm_gains, head_weight, latent_init)
        ],
        out_specs=[whole((rows, number)) for number in widths],
        out_shape=[shaped((rows, number), jnp.bfloat16) for number in widths],
        compiler_params=pltpu.CompilerParams(vmem_limit_bytes=62 * MIB),
        cost_estimate=cost(3),
        name="shards",
    )(matrices, kv_weight, norm_gains, head_weight, latent_init)


def run_join(targets, passing, after):
    moves = [move for _, parts in targets for move in parts]
    sources = []
    for array, _, _ in moves:
        if not any(array is known for known in sources):
            sources.append(array)
    where = {id(array): number for number, array in enumerate(sources)}
    count, kept = len(sources), len(passing)

    def kernel(*refs):
        outs = refs[count + kept : count + kept + len(targets)]
        for target, (_, parts) in zip(outs, targets):
            for array, cut, first in parts:
                source = refs[where[id(array)]]
                if cut is None:
                    target[first : first + source.shape[0]] = source[...]
                else:
                    target[first] = source[:, cut]

    vmem = pl.BlockSpec(memory_space=pltpu.VMEM)
    outs = launch(
        kernel,
        after,
        sources + list(passing),
        [vmem] * count + [ANY] * kept,
        out_specs=[vmem] * len(targets) + [ANY] * kept,
        out_shape=[shaped(shape, jnp.bfloat16) for shape, _ in targets]
        + [shaped(array.shape, array.dtype) for array in passing],
        input_output_aliases={count + number: len(targets) + number for number in range(kept)},
        compiler_params=pltpu.CompilerParams(vmem_limit_bytes=16 * MIB),
        cost_estimate=cost(3),
        name="join",
    )
    return outs[: len(targets)], outs[len(targets) :]


def run_fold(me, parts, after):
    depth = 4
    operands = []
    in_specs = []
    out_specs = []
    out_shape = []
    for terms, first, last, axis in parts:
        groups, rows, _ = terms[0].shape
        each = groups // depth
        for term in terms:
            if not any(term is known for known in operands):
                operands.append(term)
                in_specs.append(
                    pl.BlockSpec((each, rows, term.shape[2]), lambda z: (z, 0, 0))
                )
        block = (each, rows // 2, last - first) if axis == "x" else (1, rows, last - first)
        for _ in range(2):
            out_specs.append(pl.BlockSpec(block, lambda z: (z, 0, 0)))
            out_shape.append(shaped((block[0] * depth,) + block[1:], jnp.bfloat16))
    where = {id(term): number for number, term in enumerate(operands)}

    def kernel(me_ref, *refs):
        out = len(operands)
        mine = {"x": me_ref[0] % 2, "y": (me_ref[0] // 4) % 2}
        for terms, first, last, axis in parts:
            sources = [refs[where[id(term)]] for term in terms]
            for side in range(2):
                spot = mine[axis] if side == 0 else 1 - mine[axis]
                if axis == "x":
                    rows = sources[0].shape[1] // 2
                    cut = (slice(None), pl.ds(pl.multiple_of(spot * rows, rows), rows), slice(first, last))
                else:
                    cut = (pl.ds(spot, 1), slice(None), slice(first, last))
                refs[out][...] = lowered(sum(source[cut].astype(jnp.float32) for source in sources))
                out += 1

    outs = launch(
        kernel,
        after,
        [me] + operands,
        [SMEM] + in_specs,
        grid=(depth,),
        out_specs=out_specs,
        out_shape=out_shape,
        compiler_params=params(32),
        cost_estimate=cost(4),
        name="fold",
    )
    return [(outs[2 * number], outs[2 * number + 1]) for number in range(len(parts))]


def run_fold_z(me, parts, after):
    depth = 4
    columns = [terms[0].shape[2] for terms in parts]

    def kernel(me_ref, *refs):
        mine = me_ref[0] // 8
        outs = refs[-depth:]
        at = 0
        column = 0
        for terms, number in zip(parts, columns):
            sources = refs[at : at + len(terms)]
            at += len(terms)
            for k in range(depth):
                outs[k][:, column : column + number] = lowered(
                    sum(source[pl.ds(mine ^ k, 1)].astype(jnp.float32) for source in sources)
                )[0]
            column += number

    vmem = pl.BlockSpec(memory_space=pltpu.VMEM)
    operands = [me] + [term for terms in parts for term in terms]
    shape = shaped((parts[0][0].shape[1], sum(columns)), jnp.bfloat16)
    return launch(
        kernel,
        after,
        operands,
        [SMEM] + [vmem] * (len(operands) - 1),
        out_specs=[vmem] * depth,
        out_shape=[shape] * depth,
        compiler_params=pltpu.CompilerParams(vmem_limit_bytes=24 * MIB),
        cost_estimate=cost(3),
        name="fold_z",
    )


def run_totals(states, grad_head, channels, tokens, gains):
    rows = grad_head.shape[0]
    flat = [term for terms in states for term in terms]
    widths = [terms[0].shape[1] for terms in states]
    small = tokens + 128
    width = widths[1] // 3
    wide_channels = (widths[0] - width - small) // 2
    blocks = width + sum(widths[1:])

    def kernel(head_ref, *refs):
        mat_ref, kv_ref, gain_ref, latent_ref, square_ref = refs[len(flat) :]
        at = 0
        column = width
        square = jnp.sum(head_ref[...] * head_ref[...], axis=0, keepdims=True)
        square = jnp.sum(square, axis=1, keepdims=True)
        for number, (terms, span) in enumerate(zip(states, widths)):
            total = sum(ref[...].astype(jnp.float32) for ref in refs[at : at + len(terms)])
            at += len(terms)
            part = jnp.sum(total * total, axis=0, keepdims=True)
            square = square + jnp.sum(part, axis=1, keepdims=True)
            if number > 0:
                mat_ref[:, column : column + span] = total
                column += span
                continue
            mat_ref[:, :width] = total[:, :width]
            latent_ref[...] = total[:, width : width + tokens]
            gain_ref[...] = total[:, width + tokens : width + small].T[:gains]
            for side in range(2):
                first = width + small + side * wide_channels
                kv_ref[side * rows : (side + 1) * rows, :] = total[:, first : first + channels]
        square_ref[...] = jnp.broadcast_to(square, square_ref.shape)

    shapes = [
            shaped((rows, blocks), jnp.float32),
            shaped((2 * rows, channels), jnp.float32),
            shaped((gains, rows), jnp.float32),
            shaped((rows, tokens), jnp.float32),
            shaped((1, 128), jnp.float32),
    ]
    return pl.pallas_call(
        kernel,
        grid=(1,),
        in_specs=[whole(array.shape) for array in [grad_head] + flat],
        out_specs=[whole(shape.shape) for shape in shapes],
        out_shape=shapes,
        compiler_params=pltpu.CompilerParams(vmem_limit_bytes=32 * MIB),
        cost_estimate=cost(3),
        name="totals",
    )(grad_head, *flat)


def run_update(squares, step_count, shares, masters, firsts, seconds):
    count = len(shares)
    given = [master for master in masters if master is not None]

    def kernel(step_ref, square_ref, *refs):
        share_refs, refs = refs[:count], refs[count:]
        master_refs, refs = list(refs[: len(given)]), refs[len(given) :]
        first_refs, second_refs, outs = refs[:count], refs[count : 2 * count], refs[2 * count :]
        norm = jnp.sqrt(jnp.sum(square_ref[...], axis=0, keepdims=True))
        outs[0][...] = norm
        factor = jnp.minimum(1.0, THRESH / norm[:, 0:1])
        steps = jnp.zeros((1, 1), jnp.float32) + step_ref[0].astype(jnp.float32)
        scale = 1.0 / (1.0 - jnp.exp2(-steps))
        for number in range(count):
            clipped = share_refs[number][...] * factor
            moment_one = 0.5 * first_refs[number][...] + 0.5 * clipped
            moment_two = 0.5 * second_refs[number][...] + 0.5 * clipped * clipped
            outs[1 + 3 * number][...] = moment_one
            outs[2 + 3 * number][...] = moment_two
            if masters[number] is None:
                outs[3 + 3 * number][...] = clipped
                continue
            master = master_refs.pop(0)[...]
            outs[3 + 3 * number][...] = master - RATE * (
                moment_one * scale / (jnp.sqrt(moment_two * scale) + TINY) + DECAY * master
            )

    shapes = [shaped((1, 128), jnp.float32)]
    shapes += [shaped(share.shape, jnp.float32) for share in shares for _ in range(3)]
    operands = [step_count, squares, *shares, *given, *firsts, *seconds]
    return pl.pallas_call(
        kernel,
        grid=(1,),
        in_specs=[SMEM] + [whole(array.shape) for array in operands[1:]],
        out_specs=[whole(shape.shape) for shape in shapes],
        out_shape=shapes,
        compiler_params=pltpu.CompilerParams(vmem_limit_bytes=62 * MIB),
        cost_estimate=cost(5),
        name="update",
    )(*operands)


def digits():
    n_wide = lax.axis_size("wide")
    n_narrow = lax.axis_size("narrow")
    rest = n_wide // 2
    top = min(4, rest)
    return (
        ("z", n_narrow * n_wide // top, top),
        ("y", 2 * n_narrow, rest // top),
        ("c", n_narrow, 2),
        ("x", 1, n_narrow),
    )


def device_index():
    return lax.axis_index("wide") * lax.axis_size("narrow") + lax.axis_index("narrow")


def exchange(values, offset):
    total = lax.axis_size(AXES)
    return lax.ppermute(values, AXES, [(i, i ^ offset) for i in range(total)])


class Gather:
    def __init__(self, shard, first, left, right, plain):
        self.shard = shard
        self.first = first
        self.widths = (left, right)
        self.rows = shard.shape[0]
        self.table = {name: (stride, size) for name, stride, size in digits()}
        self.names = (("y", "x"), ("x", "y"))
        self.plain = plain

    def send_z(self):
        stride, size = self.table["z"]
        self.got = [exchange(self.shard, k * stride) for k in range(1, size)]
        return self.got

    def join(self, targets, passing, after):
        if self.plain:
            flats = []
            for _, parts in targets:
                flats.append(
                    jnp.concatenate(
                        [
                            array if array.ndim == 3 else array[None, :, cut]
                            for array, cut, _ in parts
                        ]
                    )
                )
            return flats, passing
        return run_join(targets, passing, after)

    def join_z(self, passing=(), after=()):
        stride, size = self.table["z"]
        pieces = [self.shard] + self.got
        targets = []
        at = self.first
        for width in self.widths:
            parts = [(piece, slice(at, at + width), k) for k, piece in enumerate(pieces)]
            targets.append(((size, self.rows, width), parts))
            at += width
        self.flats, passing = self.join(targets, passing, after)
        self.offsets = [[k * stride for k in range(size)]] * 2
        return passing

    def send(self, turn):
        self.got = []
        for half in range(2):
            stride, size = self.table[self.names[half][turn]]
            self.got.append([exchange(self.flats[half], k * stride) for k in range(1, size)])
        return self.got[0] + self.got[1]

    def pieces(self, turn):
        halves = []
        for half in range(2):
            stride, size = self.table[self.names[half][turn]]
            arrays = [self.flats[half]] + self.got[half]
            halves.append(
                (arrays, [[offset ^ (k * stride) for offset in self.offsets[half]] for k in range(size)])
            )
        return halves

    def join_first(self, passing=(), after=()):
        targets = []
        offsets = []
        for arrays, groups in self.pieces(0):
            count = arrays[0].shape[0]
            parts = [(array, None, k * count) for k, array in enumerate(arrays)]
            targets.append(((count * len(arrays),) + arrays[0].shape[1:], parts))
            offsets.append([offset for group in groups for offset in group])
        self.flats, passing = self.join(targets, passing, after)
        self.offsets = offsets
        return passing

    def held(self):
        return list(self.flats) + self.got[0] + self.got[1]

    def release(self, arrays):
        self.flats = arrays[:2]
        count = len(self.got[0])
        self.got = [list(arrays[2 : 2 + count]), list(arrays[2 + count :])]

    def send_across(self):
        stride = self.table["c"][0]
        self.state = []
        fresh = []
        for arrays, offsets in self.pieces(1):
            sent = [exchange(array, stride) for array in arrays]
            fresh += sent
            self.state.append(
                (
                    arrays + sent,
                    offsets + [[offset ^ stride for offset in group] for group in offsets],
                )
            )
        return fresh

    def done(self):
        halves = []
        me = device_index()
        total = lax.axis_size(AXES)
        for arrays, offsets in self.state:
            if not self.plain:
                halves.append(Half(arrays, offsets, self.rows))
            else:
                flat = jnp.concatenate(arrays)
                spots = jnp.argsort(jnp.array([o for group in offsets for o in group]) ^ me)
                flat = jnp.take(flat, spots, axis=0).reshape(1, total * self.rows, -1)
                halves.append(Half([flat], None, total * self.rows))
        return halves


class Scatter:
    def __init__(self, me, keep, send, cut, plain, extra=None):
        self.me = me
        self.keep = keep
        self.columns = keep.shape[2]
        self.cut = cut
        self.plain = plain
        self.table = {name: (stride, size) for name, stride, size in digits()}
        self.pairs = [(keep, send)] + ([extra] if extra is not None else [])
        self.names = (("x", "y"), ("y", "x"), ("y", "x"))
        self.last = keep

    def send_across(self):
        stride = self.table["c"][0]
        fresh = [exchange(send, stride) for _, send in self.pairs]
        if not self.plain:
            terms = [self.keep, fresh[0]]
            self.state = [(terms, 0, self.cut), (terms, self.cut, self.columns)]
            return fresh
        sizes = tuple(self.table[name][1] for name in ("z", "y", "x"))
        self.state = []
        for number, ((keep, _), received) in enumerate(zip(self.pairs, fresh)):
            rows = keep.shape[0] * keep.shape[1] // (sizes[0] * sizes[1] * sizes[2])
            terms = [term.reshape(sizes + (rows, keep.shape[2])) for term in (keep, received)]
            if number == 0:
                self.state.append((["z", "y", "x"], [term[..., : self.cut] for term in terms]))
                self.state.append((["z", "y", "x"], [term[..., self.cut :] for term in terms]))
            else:
                self.state.append((["z", "y", "x"], terms))
        return fresh

    def send(self, turn, after=()):
        fresh = []
        if not self.plain:
            if turn == 2:
                kept, *sends = run_fold_z(self.me, [terms for terms, _, _ in self.state], after)
                stride = self.table["z"][0]
                fresh = [exchange(send, (k + 1) * stride) for k, send in enumerate(sends)]
                self.state = [kept] + fresh
                self.last = kept
                return fresh
            names = [ways[turn] for ways in self.names]
            pairs = run_fold(
                self.me, [entry + (name,) for entry, name in zip(self.state, names)], after
            )
            self.state = []
            for (kept, send), name in zip(pairs, names):
                received = exchange(send, self.table[name][0])
                fresh.append(received)
                self.state.append(([kept, received], 0, kept.shape[2]))
            self.last = pairs[0][0]
            return fresh
        me = device_index()
        for number, (left, terms) in enumerate(self.state):
            name = (self.names[number] + ("z",))[turn]
            stride, size = self.table[name]
            mine = (me // stride) % size
            axis = left.index(name)

            def part(index):
                return lowered(
                    sum(
                        lax.dynamic_index_in_dim(term, index, axis, keepdims=False).astype(jnp.float32)
                        for term in terms
                    )
                )

            kept = part(mine)
            sent = [exchange(part(mine ^ k), k * stride) for k in range(1, size)]
            fresh += sent
            self.state[number] = ([entry for entry in left if entry != name], [kept] + sent)
            self.last = kept
        return fresh

    def done(self):
        if not self.plain:
            return sum(term.astype(jnp.float32) for term in self.state)
        sums = [sum(term.astype(jnp.float32) for term in terms) for _, terms in self.state]
        rows = sums[0].shape[0]
        if len(sums) > 2:
            sums[2:] = [sums[2][:rows], sums[2][rows:]]
        return jnp.concatenate(sums, axis=1)


def share(values):
    total = lax.axis_size(AXES)
    spread = jnp.broadcast_to(values[None], (total,) + values.shape)
    return lax.all_to_all(spread, AXES, 0, 0, tiled=True)


def on_device(
    pixels,
    labels,
    partner,
    pair_on,
    step_count,
    matrices,
    kv_weight,
    norm_gains,
    head_weight,
    latent_init,
    matrices_first,
    kv_first,
    gains_first,
    head_first,
    latent_first,
    matrices_second,
    kv_second,
    gains_second,
    head_second,
    latent_second,
):
    axis_count = lax.axis_size(AXES)
    n_narrow = lax.axis_size("narrow")
    index = device_index()
    me = jnp.stack([index, jnp.int32(n_narrow)]).astype(jnp.int32)
    micro = pixels.shape[0]
    tokens = latent_init.shape[1]
    width = matrices.shape[1] // 10
    rows = matrices.shape[0]
    channels = pixels.shape[3]
    wide_channels = -(-channels // 128) * 128
    classes = head_weight.shape[1]

    half = width // 2
    wide_half = width + half
    small_columns = tokens + 128
    plain = rows % 16 != 0 or tuple(size for _, _, size in digits()) != (4, 2, 2, 2)
    pictures = jnp.pad(pixels[:, 0], ((0, 0), (0, 0), (0, wide_channels - channels)))
    blocks = ((2, 4), (4, 7), (7, 10))
    shards = run_shards(matrices, kv_weight, norm_gains.T, head_weight, latent_init, blocks)
    chunks = [
        Gather(shards[0], 0, small_columns + width, width + 2 * wide_channels, plain),
        Gather(shards[1], 0, width, width, plain),
        Gather(shards[2], 0, wide_half, wide_half, plain),
        Gather(shards[3], 0, 2 * width, 2 * width, plain),
    ]

    def block(halves, column, last=width):
        left = halves[0].arrays[0].shape[2]
        if column >= left:
            return [(halves[1], column - left, 0, last)]
        if column + last <= left:
            return [(halves[0], column, 0, last)]
        return [(halves[0], column, 0, left - column), (halves[1], 0, left - column, last)]

    first, second, third, fourth = chunks
    first.send_z()
    second.send_z()
    (pictures,) = first.join_z([pictures])
    first.send(0)
    first.join_first()
    first.send(1)
    (third.shard,) = second.join_z([third.shard], after=first.flats)
    second.send(0)
    third.send_z()
    first.send_across()
    second.join_first()
    second.send(1)
    halves = first.done()
    weights = {0: (halves[0], small_columns), 1: (halves[1], 0)}
    small_half, kv_half = (halves[0], 0), (halves[1], width)
    if kv_half[0].offsets is None:
        array = kv_half[0].arrays[0][..., width:].reshape(axis_count, rows, 2, wide_channels)
        array = array.transpose(0, 2, 1, 3).reshape(1, 2 * width, wide_channels)
        kv_half = (Half([array], None, 2 * width), 0)
    latent_one, blended, attend, pairs, initial, hidden_zero, queries, scales = run_cross_forward(
        me, pictures, small_half, kv_half, weights[0], weights[1], width, tokens,
        after=second.flats,
    )
    second.release(second.join([], second.held(), [latent_one])[1])
    second.send_across()
    (fourth.shard,) = third.join_z([fourth.shard], after=second.flats)
    third.send(0)
    fourth.send_z()
    third.join_first(after=third.flats)
    third.send(1)
    for number in range(2):
        weights[2 + number] = (second.done()[number], 0)
    latent_two, hidden_one, active_one, steep_one = run_feed_forward(
        me, scales, latent_one, weights[2], weights[3], 2, micro, False,
        after=third.flats,
    )
    third.release(fourth.join_z(third.held(), after=[latent_two]))
    third.send_across()
    fourth.send(0)
    fourth.join_first()
    fourth.send(1)
    halves = third.done()
    for number in range(3):
        weights[4 + number] = (Joint(block(halves, number * width)), 0)
    hidden_two, packed, attend_self, blended_self = [], [], [], []
    for crop in range(micro):
        outs = run_self_forward(
            crop, me, scales, latent_two, weights[4], weights[5], weights[6], micro,
            after=fourth.flats if crop == 0 else fourth.flats,
        )
        for entries, out in zip((hidden_two, packed, attend_self, blended_self), outs):
            entries.append(out)
        if crop == 0:
            fourth.release(fourth.join([], fourth.held(), [blended_self[0]])[1])
            fourth.send_across()
    halves = fourth.done()
    weights[7], weights[8], weights[9] = (halves[0], 0), (halves[0], width), (halves[1], 0)
    result, hidden_three, active_three, steep_three, pooled, latent_three = run_feed_forward(
        me, scales, latent_two, weights[8], weights[9], 6, micro, True, (blended_self, weights[7])
    )
    marks = jnp.stack(
        [labels[:, 0] // 256, labels[:, 0] % 256, partner[:, 0] // 256, partner[:, 0] % 256, pair_on[:, 0]],
        axis=1,
    )
    marks = jnp.pad(lowered(marks), ((0, 0), (0, MARKS - marks.shape[1])))
    pooled_all = share(jnp.concatenate([pooled.reshape(micro, width), marks], axis=1))
    pooled_all = pooled_all.reshape(axis_count * micro, width + MARKS)
    loss_tile, grad_logits, grad_pooled = run_losses(
        me, pooled_all, [(halves[1], width), (halves[1], width + half)], classes, axis_count, micro
    )
    total_loss = loss_tile[0, 0]
    counts = loss_tile[1 : 1 + micro, 0].astype(jnp.int32)
    pooled_rows = lax.dynamic_slice_in_dim(pooled_all, index * rows, rows, axis=1)
    grad_head = dot_tn(pooled_rows, grad_logits)[:, :classes]

    sender = Sender(width, n_narrow * rows)
    total_tokens = micro * tokens

    def single(left, right):
        return [(left, 0, total_tokens)], [(right, 0, 0)]

    upstream, gain_high, low, before, behind = run_feed_backward(
        me, scales, latent_three, (result, grad_pooled), steep_three, weights[8], weights[9], 6, micro, True
    )
    keep, send = run_weights(
        me,
        [
            (
                [(rows_of, 0, tokens) for rows_of in blended_self],
                [(behind, crop * tokens, 0) for crop in range(micro)],
            ),
            single(hidden_three, before),
            single(active_three, low),
        ],
        sender,
    )
    one = Scatter(me, keep, send, wide_half, plain)
    one.send_across()
    grads = []
    gain_mid = 0.0
    onward = None
    for crop in range(micro):
        waits = ()
        if crop == 1:
            one.send(0, after=[onward])
            waits = [one.last]
        grad_packed, onward, gain = run_self_backward(
            crop, me, scales, latent_two, upstream, (packed[crop], attend_self[crop]),
            weights[4], weights[5], weights[6], weights[7], micro, onward, after=waits,
        )
        grads.append(grad_packed)
        gain_mid = gain_mid + gain
    upstream = onward
    one.send(1, after=[onward])
    keep, send = run_weights(
        me,
        [
            (
                [(hidden_two[crop], 0, tokens) for crop in range(micro)],
                [(grads[crop], 0, number * width) for crop in range(micro)],
            )
            for number in range(3)
        ],
        sender,
        after=[one.last],
    )
    two = Scatter(me, keep, send, wide_half, plain)
    two.send_across()
    ups, lows, befores, behinds = [], [], [], []
    gain_low = 0.0
    for crop in range(micro):
        outs = run_feed_backward(
            me, scales, latent_one, upstream, steep_one, weights[2], weights[3], 2, micro, False, crop,
            after=[keep] if crop == 0 else [two.last, one.last],
        )
        gain_low = gain_low + outs[1]
        for entries, out in zip((ups, lows, befores, behinds), (outs[0],) + tuple(outs[2:])):
            entries.append(out)
        if crop == 0:
            arriving = two.send(0, after=[outs[0]])
            one_z = one.send(2, after=[two.last])
    keep, send = run_weights(
        me,
        [
            (
                [(left, crop * tokens, tokens) for crop in range(micro)],
                [(rights[crop], 0, 0) for crop in range(micro)],
            )
            for left, rights in ((blended, behinds), (hidden_one, befores), (active_one, lows))
        ],
        sender,
        after=ups[-1:] + arriving,
    )
    three = Scatter(me, keep, send, wide_half, plain)
    three.send_across()
    two.send(1, after=[keep])
    gains = jnp.concatenate(
        [
            jnp.zeros((2, width), jnp.float32),
            gain_low[:2],
            gain_mid[:2],
            gain_high[:4],
            jnp.zeros((6, width), jnp.float32),
        ]
    )
    grad_queries, grad_pairs = [], []
    back = None
    for crop in range(micro):
        outs = run_cross_backward(
            crop, me, scales, initial, ups, (queries, attend, pairs), gains,
            weights[0], weights[1], micro, back, after=[two.last],
        )
        grad_queries.append(outs[0])
        grad_pairs.append(outs[1])
        back = outs[2]
        if crop == 0:
            arriving = three.send(0, after=[back] + one_z)
            two_z = two.send(2, after=[three.last])
    grad_small = back
    keep, send, *extra = run_last_weights(
        me, hidden_zero, grad_queries, grad_pairs, pictures, grad_small,
        sender, rows, plain, after=arriving + two_z,
    )
    four = Scatter(me, keep, send, width, plain, extra or None)
    four.send_across()
    arriving = three.send(1, after=[keep])
    four.send(0, after=arriving)
    arriving = three.send(2, after=[four.last])
    four.send(1, after=arriving)
    four.send(2)
    if plain:
        last = four.done()
        grad_matrices = jnp.concatenate(
            [last[:, :width], three.done(), two.done(), one.done()], axis=1
        )
        grad_kv = last[:, width + small_columns :]
        grad_kv = jnp.concatenate(
            [grad_kv[:, :channels], grad_kv[:, wide_channels : wide_channels + channels]]
        )
        grad_small = last[:, width : width + small_columns]
        grad_gains, grad_latent = grad_small[:, tokens : tokens + 10].T, grad_small[:, :tokens]
        shares = (grad_matrices, grad_kv, grad_gains, grad_head, grad_latent)
        square = sum(jnp.sum(member * member) for member in shares)
        square = jnp.broadcast_to(square, (1, 128))
    else:
        grad_matrices, grad_kv, grad_gains, grad_latent, square = run_totals(
            [four.state, three.state, two.state, one.state],
            grad_head,
            channels,
            tokens,
            norm_gains.shape[1],
        )
    shares = (grad_matrices, grad_kv, grad_gains, grad_head, grad_latent)
    norm, *results = run_update(
        share(square[0]),
        step_count,
        shares,
        (matrices, kv_weight, None, head_weight, None),
        (matrices_first, kv_first, gains_first.T, head_first, latent_first),
        (matrices_second, kv_second, gains_second.T, head_second, latent_second),
    )
    results[6:9] = [result.T for result in results[6:9]]
    return (total_loss, norm[0, 0], counts, *results)


def solution(mesh):
    in_specs = (
        P(None, ("wide", "narrow"), None, None),
        P(None, ("wide", "narrow")),
        P(None, ("wide", "narrow")),
        P(None, ("wide", "narrow")),
        P(),
        P(("wide", "narrow"), None),
        P(("wide", "narrow"), None),
        P(("wide", "narrow"), None),
        P(("wide", "narrow"), None),
        P(("wide", "narrow"), None),
        P(("wide", "narrow"), None),
        P(("wide", "narrow"), None),
        P(("wide", "narrow"), None),
        P(("wide", "narrow"), None),
        P(("wide", "narrow"), None),
        P(("wide", "narrow"), None),
        P(("wide", "narrow"), None),
        P(("wide", "narrow"), None),
        P(("wide", "narrow"), None),
        P(("wide", "narrow"), None),
    )
    out_specs = (
        P(),
        P(),
        P(),
        P(("wide", "narrow"), None),
        P(("wide", "narrow"), None),
        P(("wide", "narrow"), None),
        P(("wide", "narrow"), None),
        P(("wide", "narrow"), None),
        P(("wide", "narrow"), None),
        P(("wide", "narrow"), None),
        P(("wide", "narrow"), None),
        P(("wide", "narrow"), None),
        P(("wide", "narrow"), None),
        P(("wide", "narrow"), None),
        P(("wide", "narrow"), None),
        P(("wide", "narrow"), None),
        P(("wide", "narrow"), None),
        P(("wide", "narrow"), None),
    )
    return jax.shard_map(
        on_device, mesh=mesh, in_specs=in_specs, out_specs=out_specs, check_vma=False
    )
```

profile of v0, /device:TPU:0, one launch (start us, length us, event | category | flops | bytes accessed | tf_op | source)
XLA Modules:
  0.0 523.7 jit_solution(9890267972232494432)
XLA Ops:
  15.7 9.3 %collective-permute-done.1.refs_2_ = bf16[32,3456]{1,0:T(8,128)(2,1)S(1)} collective-permute-done((bf16[32,3456]{1,0:T(8,128)(2,1)}, bf16[32,3456]{1,0:T(8,128)(2,1)S(1)}, u32[]{:S(2)}, u32[]{:S(2)}) %collective-permute-start.1) | collective-permute-done | bytes 221216 | tf_op jit(solution)/shard_map/ppermute | solution.py:1238
  29.8 8.3 %collective-permute-done.3.refs_1_ = bf16[4,32,1664]{2,1,0:T(8,128)(2,1)S(1)} collective-permute-done((bf16[4,32,1664]{2,1,0:T(8,128)(2,1)S(1)}, bf16[4,32,1664]{2,1,0:T(8,128)(2,1)S(1)}, u32[]{:S(2)}, u32[]{:S(2)}) %collective-permute-start.3) | collective-permute-done | bytes 426016 | tf_op jit(solution)/shard_map/ppermute | solution.py:1238
  48.2 8.6 %collective-permute-done.8.refs_7_.refs_15_.refs_13_ = bf16[8,32,1792]{2,1,0:T(8,128)(2,1)S(1)} collective-permute-done((bf16[8,32,1792]{2,1,0:T(8,128)(2,1)S(1)}, bf16[8,32,1792]{2,1,0:T(8,128)(2,1)S(1)}, u32[]{:S(2)}, u32[]{:S(2)}) %collective-permute-start.8) | collective-permute-done | bytes 917536 | tf_op jit(solution)/shard_map/ppermute | solution.py:1238
  89.6 12.4 %cross_forward.1 = (f32[1024,1024]{1,0:T(8,128)}, bf16[1024,1024]{1,0:T(8,128)(2,1)}, f32[2,512,272]{2,1,0:T(8,128)}, bf16[2,272,2048]{2,1,0:T(8,128)(2,1)}, f32...) custom-call(s32[2]{0:T(128)S(1)} %pad_add_fusion.refs_0_, ...), custom_call_target="tpu_custom_call" | custom-call | flops 9900000256 | bytes 1024 | tf_op jit(solution)/shard_map/cross_forward/pallas_call | solution.py:146
  121.6 12.6 %feed_forward.2 = (f32[1024,1024]{1,0:T(8,128)}, bf16[1024,1024]{1,0:T(8,128)(2,1)}, bf16[1024,1024]{1,0:T(8,128)(2,1)}, bf16[1024,1024]{1,0:T(8,128)(2,1)}) custom-call(s32[2]{0:T(128)} %copy-done.20, f32[16,1024]{1,0:T(8,128)} %copy-done.18, f32[1024,1024]{1,0:T(8,128)} %get-tuple-element.199.refs_4_.refs_2_, bf16[8,32,1024]{2,1,0:T(8,128)(2,1)} %copy-done.7, ...), custom_call_target="tpu_custom_call" | custom-call | flops 9900000256 | bytes 1024 | tf_op jit(solution)/shard_map/feed_forward/pallas_call | solution.py:146
  145.2 9.3 %collective-permute-done.36.refs_1_ = bf16[4,32,2048]{2,1,0:T(8,128)(2,1)S(1)} collective-permute-done((bf16[4,32,2048]{2,1,0:T(8,128)(2,1)S(1)}, bf16[4,32,2048]{2,1,0:T(8,128)(2,1)S(1)}, u32[]{:S(2)}, u32[]{:S(2)}) %collective-permute-start.36) | collective-permute-done | bytes 524320 | tf_op jit(solution)/shard_map/ppermute | solution.py:1238
  163.2 12.9 %self_forward.2 = (bf16[512,1024]{1,0:T(8,128)(2,1)}, bf16[512,3072]{1,0:T(8,128)(2,1)}, bf16[8,512,512]{2,1,0:T(8,128)(2,1)}, bf16[512,1024]{1,0:T(8,128)(2,1)}) custom-call(s32[2]{0:T(128)} %copy-done.20, f32[16,1024]{1,0:T(8,128)} %copy-done.18, f32[1024,1024]{1,0:T(8,128)} %get-tuple-element.210.refs_8_.refs_2_, ...), custom_call_target="tpu_custom_call" | custom-call | flops 7699999744 | bytes 1024 | tf_op jit(solution)/shard_map/self_forward/pallas_call | solution.py:146
  176.1 8.8 %collective-permute-done.38.refs_2_ = bf16[8,32,2048]{2,1,0:T(8,128)(2,1)} collective-permute-done((bf16[8,32,2048]{2,1,0:T(8,128)(2,1)}, bf16[8,32,2048]{2,1,0:T(8,128)(2,1)}, u32[]{:S(2)}, u32[]{:S(2)}) %collective-permute-start.38) | collective-permute-done | bytes 1048608 | tf_op jit(solution)/shard_map/ppermute | solution.py:1238
  188.0 13.1 %self_forward.3 = (bf16[512,1024]{1,0:T(8,128)(2,1)}, bf16[512,3072]{1,0:T(8,128)(2,1)}, bf16[8,512,512]{2,1,0:T(8,128)(2,1)}, bf16[512,1024]{1,0:T(8,128)(2,1)}) custom-call(s32[2]{0:T(128)} %copy-done.20, f32[16,1024]{1,0:T(8,128)} %copy-done.18, f32[1024,1024]{1,0:T(8,128)} %get-tuple-element.210.refs_8_.refs_2_, ...), custom_call_target="tpu_custom_call" | custom-call | flops 7699999744 | bytes 1024 | tf_op jit(solution)/shard_map/self_forward/pallas_call | solution.py:146
  201.2 17.3 %feed_forward.3 = (f32[1024,1024]{1,0:T(8,128)}, bf16[1024,1024]{1,0:T(8,128)(2,1)}, bf16[1024,1024]{1,0:T(8,128)(2,1)}, bf16[1024,1024]{1,0:T(8,128)(2,1)}, bf1...) custom-call(s32[2]{0:T(128)} %copy-done.20, f32[16,1024]{1,0:T(8,128)} %copy-done.18, ...), custom_call_target="tpu_custom_call" | custom-call | flops 9900000256 | bytes 1024 | tf_op jit(solution)/shard_map/feed_forward/pallas_call | solution.py:146
  219.3 14.8 %all_to_all.13 = bf16[32,2,1152]{2,1,0:T(2,128)(2,1)S(1)} all-to-all(bf16[32,2,1152]{2,1,0:T(2,128)(2,1)S(1)} %broadcast_in_dim.8), channel_id=1, replica_groups=mesh['wide'=16,'narrow'=2] {'wide','narrow'}, dimensions={0} | all-to-all | bytes 294912 | tf_op jit(solution)/shard_map/all_to_all | solution.py:1438
  239.1 14.8 %feed_backward.3 = (f32[1024,1024]{1,0:T(8,128)}, f32[8,1024]{1,0:T(8,128)}, bf16[1024,1024]{1,0:T(8,128)(2,1)}, bf16[1024,1024]{1,0:T(8,128)(2,1)}, bf16[1024,1024]{1,0:T(8,128)(2,1)}) custom-call(s32[2]{0:T(128)} %copy-done.20, f32[16,1024]{1,0:T(8,128)} %copy-done.18, f32[1024,1024]{1,0:T(8,128)} %get-tuple-element.231.refs_2_, ...), custom_call_target="tpu_custom_call" | custom-call | flops 8800000000 | bytes 1024 | tf_op jit(solution)/shard_map/feed_backward/pallas_call | solution.py:146
  254.0 11.6 %weights.3 = (bf16[8,64,3072]{2,1,0:T(8,128)(2,1)}, bf16[8,64,3072]{2,1,0:T(8,128)(2,1)}) custom-call(s32[2]{0:T(128)} %copy-done.20, bf16[512,1024]{1,0:T(8,128)(2,1)} %get-tuple-element.220.refs_4_.refs_3_.refs_1_, bf16[512,1024]{1,0:T(8,128)(2,1)} %get-tuple-element.223.refs_4_.refs_2_, bf16[1024,1024]{1,0:T(8,128)(2,1)} %get-tuple-element.241.refs_3_, ...), custom_call_target="tpu_custom_call" | custom-call | flops 4950000128 | bytes 1024 | tf_op jit(solution)/shard_map/weights/pallas_call | solution.py:146
  265.6 18.4 %self_backward.2 = (bf16[512,3072]{1,0:T(8,128)(2,1)}, f32[1024,1024]{1,0:T(8,128)}, f32[8,1024]{1,0:T(8,128)}) custom-call(s32[2]{0:T(128)} %copy-done.20, f32[16,1024]{1,0:T(8,128)} %copy-done.18, f32[1024,1024]{1,0:T(8,128)} %get-tuple-element.210.refs_8_.refs_2_, f32[1024,1024]{1,0:T(8,128)} %get-tuple-element.235.refs_3_, ...), custom_call_target="tpu_custom_call" | custom-call | flops 11000000512 | bytes 1024 | tf_op jit(solution)/shard_map/self_backward/pallas_call | solution.py:146
  291.2 18.3 %self_backward.3 = (bf16[512,3072]{1,0:T(8,128)(2,1)}, f32[1024,1024]{1,0:T(8,128)}, f32[8,1024]{1,0:T(8,128)}) custom-call(s32[2]{0:T(128)} %copy-done.20, f32[16,1024]{1,0:T(8,128)} %copy-done.18, f32[1024,1024]{1,0:T(8,128)} %get-tuple-element.210.refs_8_.refs_2_, f32[1024,1024]{1,0:T(8,128)} %get-tuple-element.235.refs_3_, ...), custom_call_target="tpu_custom_call", output_to_operand_aliasing={{1}: (26, {})} | custom-call | flops 11000000512 | bytes 1024 | tf_op jit(solution)/shard_map/self_backward/pallas_call | solution.py:146
  314.1 12.3 %weights.4 = (bf16[8,64,3072]{2,1,0:T(8,128)(2,1)}, bf16[8,64,3072]{2,1,0:T(8,128)(2,1)}) custom-call(s32[2]{0:T(128)} %copy-done.20, bf16[512,1024]{1,0:T(8,128)(2,1)} %get-tuple-element.251.refs_1_, bf16[512,1024]{1,0:T(8,128)(2,1)} %get-tuple-element.252.refs_2_, bf16[512,3072]{1,0:T(8,128)(2,1)} %get-tuple-element.253.refs_3_, ...), custom_call_target="tpu_custom_call" | custom-call | flops 4950000128 | bytes 1024 | tf_op jit(solution)/shard_map/weights/pallas_call | solution.py:146
  329.0 9.0 %feed_backward.4 = (f32[512,1024]{1,0:T(8,128)}, f32[8,1024]{1,0:T(8,128)}, bf16[512,1024]{1,0:T(8,128)(2,1)}, bf16[512,1024]{1,0:T(8,128)(2,1)}, bf16[512,1024]{1,0:T(8,128)(2,1)}) custom-call(s32[2]{0:T(128)} %copy-done.20, f32[16,1024]{1,0:T(8,128)} %copy-done.18, f32[1024,1024]{1,0:T(8,128)} %get-tuple-element.199.refs_4_.refs_2_, ...), custom_call_target="tpu_custom_call" | custom-call | flops 4950000128 | bytes 1024 | tf_op jit(solution)/shard_map/feed_backward/pallas_call | solution.py:146
  348.6 9.1 %feed_backward.5 = (f32[512,1024]{1,0:T(8,128)}, f32[8,1024]{1,0:T(8,128)}, bf16[512,1024]{1,0:T(8,128)(2,1)}, bf16[512,1024]{1,0:T(8,128)(2,1)}, bf16[512,1024]{1,0:T(8,128)(2,1)}) custom-call(s32[2]{0:T(128)} %copy-done.20, f32[16,1024]{1,0:T(8,128)} %copy-done.18, f32[1024,1024]{1,0:T(8,128)} %get-tuple-element.199.refs_4_.refs_2_, ...), custom_call_target="tpu_custom_call" | custom-call | flops 4950000128 | bytes 1024 | tf_op jit(solution)/shard_map/feed_backward/pallas_call | solution.py:146
  364.2 11.6 %weights.5 = (bf16[8,64,3072]{2,1,0:T(8,128)(2,1)}, bf16[8,64,3072]{2,1,0:T(8,128)(2,1)}) custom-call(s32[2]{0:T(128)} %copy-done.20, bf16[1024,1024]{1,0:T(8,128)(2,1)} %get-tuple-element.278.refs_1_, bf16[512,1024]{1,0:T(8,128)(2,1)} %get-tuple-element.279.refs_2_, bf16[512,1024]{1,0:T(8,128)(2,1)} %get-tuple-element.280.refs_3_, ...), custom_call_target="tpu_custom_call" | custom-call | flops 4950000128 | bytes 1024 | tf_op jit(solution)/shard_map/weights/pallas_call | solution.py:146
  389.8 10.4 %cross_backward.2 = (bf16[512,1024]{1,0:T(8,128)(2,1)}, bf16[272,2048]{1,0:T(8,128)(2,1)}, f32[512,1024]{1,0:T(8,128)}) custom-call(s32[2]{0:T(128)S(1)} %copy-done.25, f32[16,1024]{1,0:T(8,128)S(1)} %copy-done.19, f32[512,1024]{1,0:T(8,128)} %get-tuple-element.230.refs_2_, f32[512,1024]{1,0:T(8,128)} %get-tuple-element.260.refs_3_.refs_9_, ...), custom_call_target="tpu_custom_call" | custom-call | flops 4950000128 | bytes 1024 | tf_op jit(solution)/shard_map/cross_backward/pallas_call | solution.py:146
  412.0 13.0 %cross_backward.3 = (bf16[512,1024]{1,0:T(8,128)(2,1)}, bf16[272,2048]{1,0:T(8,128)(2,1)}, bf16[1024,640]{1,0:T(8,128)(2,1)}) custom-call(s32[2]{0:T(128)S(1)} %copy-done.25, f32[16,1024]{1,0:T(8,128)S(1)} %copy-done.19, f32[512,1024]{1,0:T(8,128)} %get-tuple-element.230.refs_2_, f32[512,1024]{1,0:T(8,128)} %get-tuple-element.287.refs_10_.refs_3_, ...), custom_call_target="tpu_custom_call" | custom-call | flops 4950000128 | bytes 1024 | tf_op jit(solution)/shard_map/cross_backward/pallas_call | solution.py:146
  426.5 7.7 %last_weights.1 = (bf16[8,64,2432]{2,1,0:T(8,128)(2,1)}, bf16[8,64,2432]{2,1,0:T(8,128)(2,1)}) custom-call(s32[2]{0:T(128)S(1)} %copy-done.25, bf16[512,1024]{1,0:T(8,128)(2,1)S(1)} %copy-done.60, bf16[512,1024]{1,0:T(8,128)(2,1)S(1)} %copy-done.58, bf16[512,1024]{1,0:T(8,128)(2,1)S(1)} %copy-done.26, bf16[272,2048]{1,0:T(8,128)(2,1)} %get-tuple-element.302.refs_4_, ...), custom_call_target="tpu_custom_call" | custom-call | flops 3300000000 | bytes 1024 | tf_op jit(solution)/shard_map/last_weights/pallas_call | solution.py:146
  438.4 8.7 %collective-permute-done.64.refs_3_.refs_2_ = bf16[4,32,1536]{2,1,0:T(8,128)(2,1)S(1)} collective-permute-done((bf16[4,32,1536]{2,1,0:T(8,128)(2,1)S(1)}, bf16[4,32,1536]{2,1,0:T(8,128)(2,1)S(1)}, u32[]{:S(2)}, u32[]{:S(2)}) %collective-permute-start.64) | collective-permute-done | bytes 393248 | tf_op jit(solution)/shard_map/ppermute | solution.py:1238
  464.5 9.9 %collective-permute-done.69.refs_6_ = bf16[32,3072]{1,0:T(8,128)(2,1)S(1)} collective-permute-done((bf16[32,3072]{1,0:T(8,128)(2,1)S(1)}, bf16[32,3072]{1,0:T(8,128)(2,1)S(1)}, u32[]{:S(2)}, u32[]{:S(2)}) %collective-permute-start.69) | collective-permute-done | bytes 196640 | tf_op jit(solution)/shard_map/ppermute | solution.py:1238
  (368 shorter events, 239.0 us)
Async XLA Ops:
  48.1 37.2 %collective-permute-start.9 = (bf16[8,32,1792]{2,1,0:T(8,128)(2,1)S(1)}, bf16[8,32,1792]{2,1,0:T(8,128)(2,1)}, u32[]{:S(2)}, u32[]{:S(2)}) collective-permute-start(bf16[8,32,1792]{2,1,0:T(8,128)(2,1)S(1)} %get-tuple-element.191.refs_6_.refs_14_.refs_12_), channel_id=1, source_target_pairs={{0,2},{1,3},{2,0},{3,1},{4,6},{5,7},{6,4},{7,5},{8,10},{9,11},{10,... | collective-permute-start | bytes 2752520 | tf_op jit(solution)/shard_map/ppermute | solution.py:1238
  56.8 31.3 %collective-permute-start.10 = (bf16[8,32,1792]{2,1,0:T(8,128)(2,1)S(1)}, bf16[8,32,1792]{2,1,0:T(8,128)(2,1)}, u32[]{:S(2)}, u32[]{:S(2)}) collective-permute-start(bf16[8,32,1792]{2,1,0:T(8,128)(2,1)S(1)} %collective-permute-done.8.refs_7_.refs_15_.refs_13_), channel_id=1, source_target_pairs={{0,2},{1,3},{2,0},{3,1},{4,6},{5,7},{6,4},{7,5},{8,10},{9,11},{10,... | collective-permute-start | bytes 2752520 | tf_op jit(solution)/shard_map/ppermute | solution.py:1238
  56.8 27.4 %collective-permute-start.6 = (bf16[8,32,1664]{2,1,0:T(8,128)(2,1)S(1)}, bf16[8,32,1664]{2,1,0:T(8,128)(2,1)}, u32[]{:S(2)}, u32[]{:S(2)}) collective-permute-start(bf16[8,32,1664]{2,1,0:T(8,128)(2,1)S(1)} %get-tuple-element.190.refs_5_.refs_2_.refs_10_.refs_8_), channel_id=1, source_target_pairs={{0,2},{1,3},{2,0},{3,1},{4,6},{5,7},{6,4},{7,5},{8,10},{9,11},{10,... | collective-permute-start | bytes 2555912 | tf_op jit(solution)/shard_map/ppermute | solution.py:1238
  57.3 29.5 %collective-permute-start.7 = (bf16[8,32,1664]{2,1,0:T(8,128)(2,1)S(1)}, bf16[8,32,1664]{2,1,0:T(8,128)(2,1)}, u32[]{:S(2)}, u32[]{:S(2)}) collective-permute-start(bf16[8,32,1664]{2,1,0:T(8,128)(2,1)S(1)} %collective-permute-done.5.refs_3_.refs_11_.refs_9_), channel_id=1, source_target_pairs={{0,2},{1,3},{2,0},{3,1},{4,6},{5,7},{6,4},{7,5},{8,10},{9,11},{10,... | collective-permute-start | bytes 2555912 | tf_op jit(solution)/shard_map/ppermute | solution.py:1238
  75.6 28.6 %collective-permute-start.22 = (bf16[32,3072]{1,0:T(8,128)(2,1)}, bf16[32,3072]{1,0:T(8,128)(2,1)S(1)}, u32[]{:S(2)}, u32[]{:S(2)}) collective-permute-start(bf16[32,3072]{1,0:T(8,128)(2,1)} %copy-done.49), channel_id=1, source_target_pairs={{0,8},{1,9},{2,10},{3,11},{4,12},{5,13},{6,14},{7,15},{8,0},{9,1},... | collective-permute-start | bytes 589832 | tf_op jit(solution)/shard_map/ppermute | solution.py:1238
  84.2 20.0 %collective-permute-start.23 = (bf16[32,3072]{1,0:T(8,128)(2,1)S(1)}, bf16[32,3072]{1,0:T(8,128)(2,1)S(1)}, u32[]{:S(2)}, u32[]{:S(2)}) collective-permute-start(bf16[32,3072]{1,0:T(8,128)(2,1)S(1)} %copy-done.50), channel_id=1, source_target_pairs={{0,16},{1,17},{2,18},{3,19},{4,20},{5,21},{6,22},{7,23},{8,24},{9,... | collective-permute-start | bytes 589832 | tf_op jit(solution)/shard_map/ppermute | solution.py:1238
  113.3 20.8 %collective-permute-start.27 = (bf16[32,4096]{1,0:T(8,128)(2,1)}, bf16[32,4096]{1,0:T(8,128)(2,1)}, u32[]{:S(2)}, u32[]{:S(2)}) collective-permute-start(bf16[32,4096]{1,0:T(8,128)(2,1)} %get-tuple-element.211.refs_0_), channel_id=1, source_target_pairs={{0,8},{1,9},{2,10},{3,11},{4,12},{5,13},{6,14},{7,15},{8,0},{9,1},... | collective-permute-start | bytes 786440 | tf_op jit(solution)/shard_map/ppermute | solution.py:1238
  116.0 21.6 %collective-permute-start.28 = (bf16[32,4096]{1,0:T(8,128)(2,1)}, bf16[32,4096]{1,0:T(8,128)(2,1)S(1)}, u32[]{:S(2)}, u32[]{:S(2)}) collective-permute-start(bf16[32,4096]{1,0:T(8,128)(2,1)} %get-tuple-element.211.refs_0_), channel_id=1, source_target_pairs={{0,16},{1,17},{2,18},{3,19},{4,20},{5,21},{6,22},{7,23},{8,24},{9,... | collective-permute-start | bytes 786440 | tf_op jit(solution)/shard_map/ppermute | solution.py:1238
  118.0 19.7 %collective-permute-start.29 = (bf16[32,4096]{1,0:T(8,128)(2,1)}, bf16[32,4096]{1,0:T(8,128)(2,1)S(1)}, u32[]{:S(2)}, u32[]{:S(2)}) collective-permute-start(bf16[32,4096]{1,0:T(8,128)(2,1)} %get-tuple-element.211.refs_0_), channel_id=1, source_target_pairs={{0,24},{1,25},{2,26},{3,27},{4,28},{5,29},{6,30},{7,31},{8,16},{9,... | collective-permute-start | bytes 786440 | tf_op jit(solution)/shard_map/ppermute | solution.py:1238
  159.7 25.1 %collective-permute-start.38 = (bf16[8,32,2048]{2,1,0:T(8,128)(2,1)}, bf16[8,32,2048]{2,1,0:T(8,128)(2,1)}, u32[]{:S(2)}, u32[]{:S(2)}) collective-permute-start(bf16[8,32,2048]{2,1,0:T(8,128)(2,1)} %get-tuple-element.218.refs_19_.refs_0_), channel_id=1, source_target_pairs={{0,1},{1,0},{2,3},{3,2},{4,5},{5,4},{6,7},{7,6},{8,9},{9,8},{10,11... | collective-permute-start | bytes 3145736 | tf_op jit(solution)/shard_map/ppermute | solution.py:1238
  160.5 24.8 %collective-permute-start.39 = (bf16[8,32,2048]{2,1,0:T(8,128)(2,1)}, bf16[8,32,2048]{2,1,0:T(8,128)(2,1)}, u32[]{:S(2)}, u32[]{:S(2)}) collective-permute-start(bf16[8,32,2048]{2,1,0:T(8,128)(2,1)} %get-tuple-element.219.refs_20_.refs_1_), channel_id=1, source_target_pairs={{0,4},{1,5},{2,6},{3,7},{4,0},{5,1},{6,2},{7,3},{8,12},{9,13},{10,... | collective-permute-start | bytes 3145736 | tf_op jit(solution)/shard_map/ppermute | solution.py:1238
  290.2 19.9 %collective-permute-start.45 = (bf16[8,32,1536]{2,1,0:T(8,128)(2,1)S(1)}, bf16[8,32,1536]{2,1,0:T(8,128)(2,1)S(1)}, u32[]{:S(2)}, u32[]{:S(2)}) collective-permute-start(bf16[8,32,1536]{2,1,0:T(8,128)(2,1)S(1)} %get-tuple-element.255), channel_id=1, source_target_pairs={{0,1},{1,0},{2,3},{3,2},{4,5},{5,4},{6,7},{7,6},{8,9},{9,8},{10,11... | collective-permute-start | bytes 2359304 | tf_op jit(solution)/shard_map/ppermute | solution.py:1238
  290.5 19.6 %collective-permute-start.46 = (bf16[4,64,1536]{2,1,0:T(8,128)(2,1)S(1)}, bf16[4,64,1536]{2,1,0:T(8,128)(2,1)S(1)}, u32[]{:S(2)}, u32[]{:S(2)}) collective-permute-start(bf16[4,64,1536]{2,1,0:T(8,128)(2,1)S(1)} %get-tuple-element.257), channel_id=1, source_target_pairs={{0,4},{1,5},{2,6},{3,7},{4,0},{5,1},{6,2},{7,3},{8,12},{9,13},{10,... | collective-permute-start | bytes 2359304 | tf_op jit(solution)/shard_map/ppermute | solution.py:1238
  326.4 19.5 %collective-permute-start.48 = (bf16[4,32,1536]{2,1,0:T(8,128)(2,1)}, bf16[4,32,1536]{2,1,0:T(8,128)(2,1)}, u32[]{:S(2)}, u32[]{:S(2)}) collective-permute-start(bf16[4,32,1536]{2,1,0:T(8,128)(2,1)} %get-tuple-element.267), channel_id=1, source_target_pairs={{0,4},{1,5},{2,6},{3,7},{4,0},{5,1},{6,2},{7,3},{8,12},{9,13},{10,... | collective-permute-start | bytes 1179656 | tf_op jit(solution)/shard_map/ppermute | solution.py:1238
  344.3 19.7 %collective-permute-start.50 = (bf16[8,32,1536]{2,1,0:T(8,128)(2,1)}, bf16[8,32,1536]{2,1,0:T(8,128)(2,1)}, u32[]{:S(2)}, u32[]{:S(2)}) collective-permute-start(bf16[8,32,1536]{2,1,0:T(8,128)(2,1)} %get-tuple-element.275), channel_id=1, source_target_pairs={{0,1},{1,0},{2,3},{3,2},{4,5},{5,4},{6,7},{7,6},{8,9},{9,8},{10,11... | collective-permute-start | bytes 2359304 | tf_op jit(solution)/shard_map/ppermute | solution.py:1238
  344.7 19.4 %collective-permute-start.51 = (bf16[4,64,1536]{2,1,0:T(8,128)(2,1)}, bf16[4,64,1536]{2,1,0:T(8,128)(2,1)}, u32[]{:S(2)}, u32[]{:S(2)}) collective-permute-start(bf16[4,64,1536]{2,1,0:T(8,128)(2,1)} %get-tuple-element.277), channel_id=1, source_target_pairs={{0,4},{1,5},{2,6},{3,7},{4,0},{5,1},{6,2},{7,3},{8,12},{9,13},{10,... | collective-permute-start | bytes 2359304 | tf_op jit(solution)/shard_map/ppermute | solution.py:1238
  375.7 24.5 %collective-permute-start.54 = (bf16[8,64,3072]{2,1,0:T(8,128)(2,1)}, bf16[8,64,3072]{2,1,0:T(8,128)(2,1)}, u32[]{:S(2)}, u32[]{:S(2)}) collective-permute-start(bf16[8,64,3072]{2,1,0:T(8,128)(2,1)} %get-tuple-element.295), channel_id=1, source_target_pairs={{0,2},{1,3},{2,0},{3,1},{4,6},{5,7},{6,4},{7,5},{8,10},{9,11},{10,... | collective-permute-start | bytes 9437192 | tf_op jit(solution)/shard_map/ppermute | solution.py:1238
  377.2 23.0 %collective-permute-start.56 = (bf16[32,3072]{1,0:T(8,128)(2,1)}, bf16[32,3072]{1,0:T(8,128)(2,1)S(1)}, u32[]{:S(2)}, u32[]{:S(2)}) collective-permute-start(bf16[32,3072]{1,0:T(8,128)(2,1)} %get-tuple-element.297), channel_id=1, source_target_pairs={{0,16},{1,17},{2,18},{3,19},{4,20},{5,21},{6,22},{7,23},{8,24},{9,... | collective-permute-start | bytes 589832 | tf_op jit(solution)/shard_map/ppermute | solution.py:1238
  378.6 21.6 %collective-permute-start.57 = (bf16[32,3072]{1,0:T(8,128)(2,1)}, bf16[32,3072]{1,0:T(8,128)(2,1)S(1)}, u32[]{:S(2)}, u32[]{:S(2)}) collective-permute-start(bf16[32,3072]{1,0:T(8,128)(2,1)} %get-tuple-element.298), channel_id=1, source_target_pairs={{0,24},{1,25},{2,26},{3,27},{4,28},{5,29},{6,30},{7,31},{8,16},{9,... | collective-permute-start | bytes 589832 | tf_op jit(solution)/shard_map/ppermute | solution.py:1238
  386.9 19.9 %collective-permute-start.52 = (bf16[4,32,1536]{2,1,0:T(8,128)(2,1)S(1)}, bf16[4,32,1536]{2,1,0:T(8,128)(2,1)S(1)}, u32[]{:S(2)}, u32[]{:S(2)}) collective-permute-start(bf16[4,32,1536]{2,1,0:T(8,128)(2,1)S(1)} %get-tuple-element.292), channel_id=1, source_target_pairs={{0,4},{1,5},{2,6},{3,7},{4,0},{5,1},{6,2},{7,3},{8,12},{9,13},{10,... | collective-permute-start | bytes 1179656 | tf_op jit(solution)/shard_map/ppermute | solution.py:1238
  405.5 19.6 %collective-permute-start.58 = (bf16[8,32,1536]{2,1,0:T(8,128)(2,1)S(1)}, bf16[8,32,1536]{2,1,0:T(8,128)(2,1)S(1)}, u32[]{:S(2)}, u32[]{:S(2)}) collective-permute-start(bf16[8,32,1536]{2,1,0:T(8,128)(2,1)S(1)} %get-tuple-element.305), channel_id=1, source_target_pairs={{0,1},{1,0},{2,3},{3,2},{4,5},{5,4},{6,7},{7,6},{8,9},{9,8},{10,11... | collective-permute-start | bytes 2359304 | tf_op jit(solution)/shard_map/ppermute | solution.py:1238
  406.0 19.2 %collective-permute-start.59 = (bf16[4,64,1536]{2,1,0:T(8,128)(2,1)S(1)}, bf16[4,64,1536]{2,1,0:T(8,128)(2,1)S(1)}, u32[]{:S(2)}, u32[]{:S(2)}) collective-permute-start(bf16[4,64,1536]{2,1,0:T(8,128)(2,1)S(1)} %get-tuple-element.306), channel_id=1, source_target_pairs={{0,4},{1,5},{2,6},{3,7},{4,0},{5,1},{6,2},{7,3},{8,12},{9,13},{10,... | collective-permute-start | bytes 2359304 | tf_op jit(solution)/shard_map/ppermute | solution.py:1238
  452.1 22.3 %collective-permute-start.67 = (bf16[4,64,1408]{2,1,0:T(8,128)(2,1)S(1)}, bf16[4,64,1408]{2,1,0:T(8,128)(2,1)S(1)}, u32[]{:S(2)}, u32[]{:S(2)}) collective-permute-start(bf16[4,64,1408]{2,1,0:T(8,128)(2,1)S(1)} %get-tuple-element.318), channel_id=1, source_target_pairs={{0,4},{1,5},{2,6},{3,7},{4,0},{5,1},{6,2},{7,3},{8,12},{9,13},{10,... | collective-permute-start | bytes 2162696 | tf_op jit(solution)/shard_map/ppermute | solution.py:1238
  453.0 21.4 %collective-permute-start.66 = (bf16[8,32,1024]{2,1,0:T(8,128)(2,1)S(1)}, bf16[8,32,1024]{2,1,0:T(8,128)(2,1)S(1)}, u32[]{:S(2)}, u32[]{:S(2)}) collective-permute-start(bf16[8,32,1024]{2,1,0:T(8,128)(2,1)S(1)} %get-tuple-element.316), channel_id=1, source_target_pairs={{0,1},{1,0},{2,3},{3,2},{4,5},{5,4},{6,7},{7,6},{8,9},{9,8},{10,11... | collective-permute-start | bytes 1572872 | tf_op jit(solution)/shard_map/ppermute | solution.py:1238
  (139 other events, 1277.3 us)
where the time goes:
time: 532 us; the launch traced here: 524 us
  Pallas kernels  250 us (47%)
  waiting for transfers between devices  131 us (25%)
  starting transfers between devices  86 us (16%)
  local copies, waits for them, and re-layouts  35.8 us (7%)
  blocking collectives  14.8 us (3%)
    pallas_call x39, Pallas kernels, launch(): pl.pallas_call(inner, in_specs=list(in_specs) + [ANY] * extra, **rest)  240 us
    ppermute x76, waiting for transfers between devices, exchange(): return lax.ppermute(values, AXES, [(i, i ^ offset) for i in range(total)])  125 us
    ppermute x76, starting transfers between devices, exchange(): return lax.ppermute(values, AXES, [(i, i ^ offset) for i in range(total)])  82.3 us
    unnamed x176, local copies, waits for them, and re-layouts  34.2 us
    all_to_all x1, blocking collectives, share(): return lax.all_to_all(spread, AXES, 0, 0, tiled=True)  14.8 us
  transfers between devices with their start and end apart: 77, of which 28 were waited for; matrix products, arithmetic and copies ran while one was open for 1% of the time, Pallas kernels for 29%

commit v1 on v0

--- a/solution.py
+++ b/solution.py
@@ -833,9 +833,18 @@
             others, refs = refs[: micro - 1], refs[micro - 1 :]
         first_refs, refs = refs[: counts[0]], refs[counts[0] :]
         second_refs, refs = refs[: counts[1]], refs[counts[1] :]
-        query_out, pair_out, back_ref, first_s, second_s, sems = refs
+        query_out, pair_out, back_ref, first_s, second_s, *held, sems = refs
         second[0].start(second_refs, me_ref[0], second_s, sems.at[1], second[1])
         first[0].start(first_refs, me_ref[0], first_s, sems.at[0], first[1])
+        later = []
+        if last:
+            sources = [initial_ref, before_ref, *others]
+            later = [
+                pltpu.make_async_copy(source, target, sems.at[2 + number])
+                for number, (source, target) in enumerate(zip(sources, held))
+            ]
+        for copy in later:
+            copy.start()
         keys, values = pair_ref[0, :, :width], pair_ref[0, :, width:]
         attend = attend_ref[0]
         arrived(second_s, sems.at[1])
@@ -846,13 +855,13 @@
         pair_out[:, width:] = lowered(dot_tn(lowered(attend), blend))
         arrived(first_s, sems.at[0])
         back = dot_nt(query_out[...], first_s[...])
-        if before is not None:
-            back = before_ref[...] + back
         if not last:
-            back_ref[...] = back
+            back_ref[...] = back if before is None else before_ref[...] + back
             return
-        back, gain, bias = norm_back(initial_ref[...], scale_ref, 0, back)
-        for other in (up_ref, *others):
+        for copy in later:
+            copy.wait()
+        back, gain, bias = norm_back(held[0][...], scale_ref, 0, held[1][...] + back)
+        for other in (up_ref, *held[2:]):
             back = back + other[...]
         gains_all = jnp.concatenate(
             [gain, bias, gains_ref[2:, :], jnp.zeros((128 - gains_ref.shape[0], width), jnp.float32)], axis=0
@@ -875,14 +884,14 @@
         [
             SMEM,
             whole((16, width)),
-            whole((tokens, width)),
+            ANY,
             whole((tokens, width)),
             whole((tokens, width)),
             pl.BlockSpec((1, tokens, spots), lambda i: (crop, 0, 0)),
             pl.BlockSpec((1, spots, 2 * width), lambda i: (crop, 0, 0)),
             whole((16, width)),
         ]
-        + [whole((tokens, width))] * len(extra)
+        + [ANY if last else whole((tokens, width))] * len(extra)
         + [ANY] * sum(counts),
         grid=(1,),
         out_specs=[whole((tokens, width)), whole((spots, 2 * width)), whole(back_shape.shape)],
@@ -894,8 +903,9 @@
         scratch_shapes=[
             VMEM((width, width), jnp.bfloat16),
             VMEM((width, width), jnp.bfloat16),
-            pltpu.SemaphoreType.DMA((2,)),
-        ],
+        ]
+        + [VMEM((tokens, width), jnp.float32)] * (1 + len(extra) if last else 0)
+        + [pltpu.SemaphoreType.DMA((3 + len(extra),))],
         compiler_params=params(48),
         cost_estimate=cost(9),
         name="cross_backward",
@@ -911,11 +921,19 @@
 
     def kernel(me_ref, hidden_ref, *refs):
         query_refs, pair_refs = refs[:micro], refs[micro : 2 * micro]
-        pic_ref, small_ref, keep, send = refs[2 * micro : 2 * micro + 4]
+        pic_any, small_any, keep, send = refs[2 * micro : 2 * micro + 4]
         refs = refs[2 * micro + 4 :]
-        mat_s, kv_s, sems = refs[-3:]
+        mat_s, kv_s, pic_ref, small_ref, *pair_held, sems = refs[-5 - micro :]
+        later = [
+            pltpu.make_async_copy(source, target, sems.at[3 + number])
+            for number, (source, target) in enumerate(
+                zip((small_any, pic_any, *pair_refs), (small_ref, pic_ref, *pair_held))
+            )
+        ]
+        for copy in later:
+            copy.start()
+        pair_refs = pair_held
         core = (me_ref[0] // me_ref[1]) % 2
-        sender.start(small_ref, core, keep, send, width, sems.at[2])
         span = width // 2
         for number in range(2):
             cut = slice(number * span, (number + 1) * span)
@@ -925,6 +943,9 @@
                 )
             )
         sender.start(mat_s, core, keep, send, 0, sems.at[0])
+        for copy in later:
+            copy.wait()
+        sender.start(small_ref, core, keep, send, width, sems.at[2])
         kv_s[...] = lowered(sum(dot_tn(pair_refs[crop][...], pic_ref[crop]) for crop in range(micro)))
         if apart:
             kv_sender.start(kv_s, core, refs[0], refs[1], 0, sems.at[1])
@@ -946,15 +967,18 @@
         kernel,
         after,
         operands,
-        [SMEM] + [whole(array.shape) for array in operands[1:]],
+        [SMEM] + [whole(array.shape) for array in operands[1 : 2 + micro]] + [ANY] * (micro + 2),
         grid=(1,),
         out_specs=[ANY] * len(shapes),
         out_shape=shapes,
         scratch_shapes=[
             VMEM((width, width), jnp.bfloat16),
             VMEM((2 * width, channels), jnp.bfloat16),
-            pltpu.SemaphoreType.DMA((3,)),
-        ],
+            VMEM(pictures.shape, jnp.bfloat16),
+            VMEM(small.shape, jnp.bfloat16),
+        ]
+        + [VMEM(array.shape, jnp.bfloat16) for array in grad_pairs]
+        + [pltpu.SemaphoreType.DMA((5 + micro,))],
         compiler_params=pltpu.CompilerParams(vmem_limit_bytes=BIG * MIB),
         cost_estimate=cost(6),
         name="last_weights",
@@ -1678,7 +1702,7 @@
         me, hidden_zero, grad_queries, grad_pairs, pictures, grad_small,
         sender, rows, plain, after=arriving + two_z,
     )
-    four = Scatter(me, keep, send, width, plain, extra or None)
+    four = Scatter(me, keep, send, 128 * round(keep.shape[2] / 256), plain, extra or None)
     four.send_across()
     arriving = three.send(1, after=[keep])
     four.send(0, after=arriving)

time: 532 us -> 532 us (level)
    unnamed x176 -> x172, local copies, waits for them, and re-layouts: 34.2 us -> 34.7 us
  transfers between devices with their start and end apart: 77 -> 77, of which waited for: 28 -> 28; matrix products, arithmetic and copies ran while one was open for 1% -> 1% of each run, Pallas kernels for 29% -> 28%
where the time goes in v1:
time: 532 us; the launch traced here: 523 us
  Pallas kernels  248 us (47%)
  waiting for transfers between devices  132 us (25%)
  starting transfers between devices  86.3 us (16%)
  local copies, waits for them, and re-layouts  36.4 us (7%)
  blocking collectives  14.6 us (3%)
    pallas_call x39, Pallas kernels, launch(): pl.pallas_call(inner, in_specs=list(in_specs) + [ANY] * extra, **rest)  239 us
    ppermute x76, waiting for transfers between devices, exchange(): return lax.ppermute(values, AXES, [(i, i ^ offset) for i in range(total)])  126 us
    ppermute x76, starting transfers between devices, exchange(): return lax.ppermute(values, AXES, [(i, i ^ offset) for i in range(total)])  82.2 us
    unnamed x172, local copies, waits for them, and re-layouts  34.7 us
    all_to_all x1, blocking collectives, share(): return lax.all_to_all(spread, AXES, 0, 0, tiled=True)  14.6 us
  transfers between devices with their start and end apart: 77, of which 28 were waited for; matrix products, arithmetic and copies ran while one was open for 1% of the time, Pallas kernels for 28%

profile of v1, /device:TPU:0, one launch (start us, length us, event | category | flops | bytes accessed | tf_op | source)
XLA Modules:
  0.0 523.1 jit_solution(7938961338138392726)
XLA Ops:
  15.7 9.3 %collective-permute-done.1.refs_2_ = bf16[32,3456]{1,0:T(8,128)(2,1)S(1)} collective-permute-done((bf16[32,3456]{1,0:T(8,128)(2,1)}, bf16[32,3456]{1,0:T(8,128)(2,1)S(1)}, u32[]{:S(2)}, u32[]{:S(2)}) %collective-permute-start.1) | collective-permute-done | bytes 221216 | tf_op jit(solution)/shard_map/ppermute | solution.py:1262
  29.8 8.3 %collective-permute-done.3.refs_1_ = bf16[4,32,1664]{2,1,0:T(8,128)(2,1)S(1)} collective-permute-done((bf16[4,32,1664]{2,1,0:T(8,128)(2,1)S(1)}, bf16[4,32,1664]{2,1,0:T(8,128)(2,1)S(1)}, u32[]{:S(2)}, u32[]{:S(2)}) %collective-permute-start.3) | collective-permute-done | bytes 426016 | tf_op jit(solution)/shard_map/ppermute | solution.py:1262
  48.1 8.6 %collective-permute-done.8.refs_7_.refs_15_.refs_13_ = bf16[8,32,1792]{2,1,0:T(8,128)(2,1)S(1)} collective-permute-done((bf16[8,32,1792]{2,1,0:T(8,128)(2,1)S(1)}, bf16[8,32,1792]{2,1,0:T(8,128)(2,1)S(1)}, u32[]{:S(2)}, u32[]{:S(2)}) %collective-permute-start.8) | collective-permute-done | bytes 917536 | tf_op jit(solution)/shard_map/ppermute | solution.py:1262
  68.1 7.6 %collective-permute-done.15.refs_3_ = bf16[4,32,1024]{2,1,0:T(8,128)(2,1)} collective-permute-done((bf16[4,32,1024]{2,1,0:T(8,128)(2,1)}, bf16[4,32,1024]{2,1,0:T(8,128)(2,1)}, u32[]{:S(2)}, u32[]{:S(2)}) %collective-permute-start.15) | collective-permute-done | bytes 262176 | tf_op jit(solution)/shard_map/ppermute | solution.py:1262
  89.6 12.4 %cross_forward.1 = (f32[1024,1024]{1,0:T(8,128)}, bf16[1024,1024]{1,0:T(8,128)(2,1)}, f32[2,512,272]{2,1,0:T(8,128)}, bf16[2,272,2048]{2,1,0:T(8,128)(2,1)}, f32...) custom-call(s32[2]{0:T(128)S(1)} %pad_add_fusion.refs_0_, ...), custom_call_target="tpu_custom_call" | custom-call | flops 9900000256 | bytes 1024 | tf_op jit(solution)/shard_map/cross_forward/pallas_call | solution.py:146
  121.5 12.6 %feed_forward.2 = (f32[1024,1024]{1,0:T(8,128)}, bf16[1024,1024]{1,0:T(8,128)(2,1)}, bf16[1024,1024]{1,0:T(8,128)(2,1)}, bf16[1024,1024]{1,0:T(8,128)(2,1)}) custom-call(s32[2]{0:T(128)} %copy-done.20, f32[16,1024]{1,0:T(8,128)} %copy-done.18, f32[1024,1024]{1,0:T(8,128)} %get-tuple-element.199.refs_4_.refs_2_, bf16[8,32,1024]{2,1,0:T(8,128)(2,1)} %copy-done.7, ...), custom_call_target="tpu_custom_call" | custom-call | flops 9900000256 | bytes 1024 | tf_op jit(solution)/shard_map/feed_forward/pallas_call | solution.py:146
  145.2 9.3 %collective-permute-done.36.refs_1_ = bf16[4,32,2048]{2,1,0:T(8,128)(2,1)S(1)} collective-permute-done((bf16[4,32,2048]{2,1,0:T(8,128)(2,1)S(1)}, bf16[4,32,2048]{2,1,0:T(8,128)(2,1)S(1)}, u32[]{:S(2)}, u32[]{:S(2)}) %collective-permute-start.36) | collective-permute-done | bytes 524320 | tf_op jit(solution)/shard_map/ppermute | solution.py:1262
  163.2 12.9 %self_forward.2 = (bf16[512,1024]{1,0:T(8,128)(2,1)}, bf16[512,3072]{1,0:T(8,128)(2,1)}, bf16[8,512,512]{2,1,0:T(8,128)(2,1)}, bf16[512,1024]{1,0:T(8,128)(2,1)}) custom-call(s32[2]{0:T(128)} %copy-done.20, f32[16,1024]{1,0:T(8,128)} %copy-done.18, f32[1024,1024]{1,0:T(8,128)} %get-tuple-element.210.refs_8_.refs_2_, ...), custom_call_target="tpu_custom_call" | custom-call | flops 7699999744 | bytes 1024 | tf_op jit(solution)/shard_map/self_forward/pallas_call | solution.py:146
  176.0 8.8 %collective-permute-done.38.refs_2_ = bf16[8,32,2048]{2,1,0:T(8,128)(2,1)} collective-permute-done((bf16[8,32,2048]{2,1,0:T(8,128)(2,1)}, bf16[8,32,2048]{2,1,0:T(8,128)(2,1)}, u32[]{:S(2)}, u32[]{:S(2)}) %collective-permute-start.38) | collective-permute-done | bytes 1048608 | tf_op jit(solution)/shard_map/ppermute | solution.py:1262
  188.0 13.3 %self_forward.3 = (bf16[512,1024]{1,0:T(8,128)(2,1)}, bf16[512,3072]{1,0:T(8,128)(2,1)}, bf16[8,512,512]{2,1,0:T(8,128)(2,1)}, bf16[512,1024]{1,0:T(8,128)(2,1)}) custom-call(s32[2]{0:T(128)} %copy-done.20, f32[16,1024]{1,0:T(8,128)} %copy-done.18, f32[1024,1024]{1,0:T(8,128)} %get-tuple-element.210.refs_8_.refs_2_, ...), custom_call_target="tpu_custom_call" | custom-call | flops 7699999744 | bytes 1024 | tf_op jit(solution)/shard_map/self_forward/pallas_call | solution.py:146
  201.4 17.3 %feed_forward.3 = (f32[1024,1024]{1,0:T(8,128)}, bf16[1024,1024]{1,0:T(8,128)(2,1)}, bf16[1024,1024]{1,0:T(8,128)(2,1)}, bf16[1024,1024]{1,0:T(8,128)(2,1)}, bf1...) custom-call(s32[2]{0:T(128)} %copy-done.20, f32[16,1024]{1,0:T(8,128)} %copy-done.18, ...), custom_call_target="tpu_custom_call" | custom-call | flops 9900000256 | bytes 1024 | tf_op jit(solution)/shard_map/feed_forward/pallas_call | solution.py:146
  219.5 14.6 %all_to_all.13 = bf16[32,2,1152]{2,1,0:T(2,128)(2,1)S(1)} all-to-all(bf16[32,2,1152]{2,1,0:T(2,128)(2,1)S(1)} %broadcast_in_dim.8), channel_id=1, replica_groups=mesh['wide'=16,'narrow'=2] {'wide','narrow'}, dimensions={0} | all-to-all | bytes 294912 | tf_op jit(solution)/shard_map/all_to_all | solution.py:1462
  239.1 14.9 %feed_backward.3 = (f32[1024,1024]{1,0:T(8,128)}, f32[8,1024]{1,0:T(8,128)}, bf16[1024,1024]{1,0:T(8,128)(2,1)}, bf16[1024,1024]{1,0:T(8,128)(2,1)}, bf16[1024,1024]{1,0:T(8,128)(2,1)}) custom-call(s32[2]{0:T(128)} %copy-done.20, f32[16,1024]{1,0:T(8,128)} %copy-done.18, f32[1024,1024]{1,0:T(8,128)} %get-tuple-element.231.refs_2_, ...), custom_call_target="tpu_custom_call" | custom-call | flops 8800000000 | bytes 1024 | tf_op jit(solution)/shard_map/feed_backward/pallas_call | solution.py:146
  253.9 11.5 %weights.3 = (bf16[8,64,3072]{2,1,0:T(8,128)(2,1)}, bf16[8,64,3072]{2,1,0:T(8,128)(2,1)}) custom-call(s32[2]{0:T(128)} %copy-done.20, bf16[512,1024]{1,0:T(8,128)(2,1)} %get-tuple-element.220.refs_4_.refs_3_.refs_1_, bf16[512,1024]{1,0:T(8,128)(2,1)} %get-tuple-element.223.refs_4_.refs_2_, bf16[1024,1024]{1,0:T(8,128)(2,1)} %get-tuple-element.241.refs_3_, ...), custom_call_target="tpu_custom_call" | custom-call | flops 4950000128 | bytes 1024 | tf_op jit(solution)/shard_map/weights/pallas_call | solution.py:146
  265.5 18.4 %self_backward.2 = (bf16[512,3072]{1,0:T(8,128)(2,1)}, f32[1024,1024]{1,0:T(8,128)}, f32[8,1024]{1,0:T(8,128)}) custom-call(s32[2]{0:T(128)} %copy-done.20, f32[16,1024]{1,0:T(8,128)} %copy-done.18, f32[1024,1024]{1,0:T(8,128)} %get-tuple-element.210.refs_8_.refs_2_, f32[1024,1024]{1,0:T(8,128)} %get-tuple-element.235.refs_3_, ...), custom_call_target="tpu_custom_call" | custom-call | flops 11000000512 | bytes 1024 | tf_op jit(solution)/shard_map/self_backward/pallas_call | solution.py:146
  291.2 18.3 %self_backward.3 = (bf16[512,3072]{1,0:T(8,128)(2,1)}, f32[1024,1024]{1,0:T(8,128)}, f32[8,1024]{1,0:T(8,128)}) custom-call(s32[2]{0:T(128)} %copy-done.20, f32[16,1024]{1,0:T(8,128)} %copy-done.18, f32[1024,1024]{1,0:T(8,128)} %get-tuple-element.210.refs_8_.refs_2_, f32[1024,1024]{1,0:T(8,128)} %get-tuple-element.235.refs_3_, ...), custom_call_target="tpu_custom_call", output_to_operand_aliasing={{1}: (26, {})} | custom-call | flops 11000000512 | bytes 1024 | tf_op jit(solution)/shard_map/self_backward/pallas_call | solution.py:146
  314.1 12.3 %weights.4 = (bf16[8,64,3072]{2,1,0:T(8,128)(2,1)}, bf16[8,64,3072]{2,1,0:T(8,128)(2,1)}) custom-call(s32[2]{0:T(128)} %copy-done.20, bf16[512,1024]{1,0:T(8,128)(2,1)} %get-tuple-element.251.refs_1_, bf16[512,1024]{1,0:T(8,128)(2,1)} %get-tuple-element.252.refs_2_, bf16[512,3072]{1,0:T(8,128)(2,1)} %get-tuple-element.253.refs_3_, ...), custom_call_target="tpu_custom_call" | custom-call | flops 4950000128 | bytes 1024 | tf_op jit(solution)/shard_map/weights/pallas_call | solution.py:146
  329.0 9.0 %feed_backward.4 = (f32[512,1024]{1,0:T(8,128)}, f32[8,1024]{1,0:T(8,128)}, bf16[512,1024]{1,0:T(8,128)(2,1)}, bf16[512,1024]{1,0:T(8,128)(2,1)}, bf16[512,1024]{1,0:T(8,128)(2,1)}) custom-call(s32[2]{0:T(128)} %copy-done.20, f32[16,1024]{1,0:T(8,128)} %copy-done.18, f32[1024,1024]{1,0:T(8,128)} %get-tuple-element.199.refs_4_.refs_2_, ...), custom_call_target="tpu_custom_call" | custom-call | flops 4950000128 | bytes 1024 | tf_op jit(solution)/shard_map/feed_backward/pallas_call | solution.py:146
  348.7 9.1 %feed_backward.5 = (f32[512,1024]{1,0:T(8,128)}, f32[8,1024]{1,0:T(8,128)}, bf16[512,1024]{1,0:T(8,128)(2,1)}, bf16[512,1024]{1,0:T(8,128)(2,1)}, bf16[512,1024]{1,0:T(8,128)(2,1)}) custom-call(s32[2]{0:T(128)} %copy-done.20, f32[16,1024]{1,0:T(8,128)} %copy-done.18, f32[1024,1024]{1,0:T(8,128)} %get-tuple-element.199.refs_4_.refs_2_, ...), custom_call_target="tpu_custom_call" | custom-call | flops 4950000128 | bytes 1024 | tf_op jit(solution)/shard_map/feed_backward/pallas_call | solution.py:146
  364.1 11.5 %weights.5 = (bf16[8,64,3072]{2,1,0:T(8,128)(2,1)}, bf16[8,64,3072]{2,1,0:T(8,128)(2,1)}) custom-call(s32[2]{0:T(128)} %copy-done.20, bf16[1024,1024]{1,0:T(8,128)(2,1)} %get-tuple-element.278.refs_1_, bf16[512,1024]{1,0:T(8,128)(2,1)} %get-tuple-element.279.refs_2_, bf16[512,1024]{1,0:T(8,128)(2,1)} %get-tuple-element.280.refs_3_, ...), custom_call_target="tpu_custom_call" | custom-call | flops 4950000128 | bytes 1024 | tf_op jit(solution)/shard_map/weights/pallas_call | solution.py:146
  389.8 9.8 %cross_backward.2 = (bf16[512,1024]{1,0:T(8,128)(2,1)}, bf16[272,2048]{1,0:T(8,128)(2,1)}, f32[512,1024]{1,0:T(8,128)}) custom-call(s32[2]{0:T(128)S(1)} %copy-done.25, f32[16,1024]{1,0:T(8,128)S(1)} %copy-done.19, f32[512,1024]{1,0:T(8,128)} %get-tuple-element.230.refs_2_, f32[512,1024]{1,0:T(8,128)} %get-tuple-element.260.refs_3_.refs_9_, ...), custom_call_target="tpu_custom_call" | custom-call | flops 4950000128 | bytes 1024 | tf_op jit(solution)/shard_map/cross_backward/pallas_call | solution.py:146
  411.4 11.8 %cross_backward.3 = (bf16[512,1024]{1,0:T(8,128)(2,1)}, bf16[272,2048]{1,0:T(8,128)(2,1)}, bf16[1024,640]{1,0:T(8,128)(2,1)}) custom-call(s32[2]{0:T(128)S(1)} %copy-done.25, f32[16,1024]{1,0:T(8,128)S(1)} %copy-done.19, f32[512,1024]{1,0:T(8,128)} %get-tuple-element.230.refs_2_, f32[512,1024]{1,0:T(8,128)} %get-tuple-element.287.refs_10_.refs_3_, ...), custom_call_target="tpu_custom_call" | custom-call | flops 4950000128 | bytes 1024 | tf_op jit(solution)/shard_map/cross_backward/pallas_call | solution.py:146
  436.5 8.8 %collective-permute-done.64.refs_3_.refs_2_ = bf16[4,32,1536]{2,1,0:T(8,128)(2,1)S(1)} collective-permute-done((bf16[4,32,1536]{2,1,0:T(8,128)(2,1)S(1)}, bf16[4,32,1536]{2,1,0:T(8,128)(2,1)S(1)}, u32[]{:S(2)}, u32[]{:S(2)}) %collective-permute-start.64) | collective-permute-done | bytes 393248 | tf_op jit(solution)/shard_map/ppermute | solution.py:1262
  463.6 9.9 %collective-permute-done.69.refs_6_ = bf16[32,3072]{1,0:T(8,128)(2,1)S(1)} collective-permute-done((bf16[32,3072]{1,0:T(8,128)(2,1)S(1)}, bf16[32,3072]{1,0:T(8,128)(2,1)S(1)}, u32[]{:S(2)}, u32[]{:S(2)}) %collective-permute-start.69) | collective-permute-done | bytes 196640 | tf_op jit(solution)/shard_map/ppermute | solution.py:1262
  (364 shorter events, 240.2 us)
Async XLA Ops:
  6.1 18.9 %collective-permute-start.1 = (bf16[32,3456]{1,0:T(8,128)(2,1)}, bf16[32,3456]{1,0:T(8,128)(2,1)S(1)}, u32[]{:S(2)}, u32[]{:S(2)}) collective-permute-start(bf16[32,3456]{1,0:T(8,128)(2,1)} %get-tuple-element.186.refs_0_), channel_id=1, source_target_pairs={{0,16},{1,17},{2,18},{3,19},{4,20},{5,21},{6,22},{7,23},{8,24},{9,... | collective-permute-start | bytes 663560 | tf_op jit(solution)/shard_map/ppermute | solution.py:1262
  48.1 37.2 %collective-permute-start.9 = (bf16[8,32,1792]{2,1,0:T(8,128)(2,1)S(1)}, bf16[8,32,1792]{2,1,0:T(8,128)(2,1)}, u32[]{:S(2)}, u32[]{:S(2)}) collective-permute-start(bf16[8,32,1792]{2,1,0:T(8,128)(2,1)S(1)} %get-tuple-element.191.refs_6_.refs_14_.refs_12_), channel_id=1, source_target_pairs={{0,2},{1,3},{2,0},{3,1},{4,6},{5,7},{6,4},{7,5},{8,10},{9,11},{10,... | collective-permute-start | bytes 2752520 | tf_op jit(solution)/shard_map/ppermute | solution.py:1262
  56.8 31.3 %collective-permute-start.10 = (bf16[8,32,1792]{2,1,0:T(8,128)(2,1)S(1)}, bf16[8,32,1792]{2,1,0:T(8,128)(2,1)}, u32[]{:S(2)}, u32[]{:S(2)}) collective-permute-start(bf16[8,32,1792]{2,1,0:T(8,128)(2,1)S(1)} %collective-permute-done.8.refs_7_.refs_15_.refs_13_), channel_id=1, source_target_pairs={{0,2},{1,3},{2,0},{3,1},{4,6},{5,7},{6,4},{7,5},{8,10},{9,11},{10,... | collective-permute-start | bytes 2752520 | tf_op jit(solution)/shard_map/ppermute | solution.py:1262
  56.8 27.4 %collective-permute-start.6 = (bf16[8,32,1664]{2,1,0:T(8,128)(2,1)S(1)}, bf16[8,32,1664]{2,1,0:T(8,128)(2,1)}, u32[]{:S(2)}, u32[]{:S(2)}) collective-permute-start(bf16[8,32,1664]{2,1,0:T(8,128)(2,1)S(1)} %get-tuple-element.190.refs_5_.refs_2_.refs_10_.refs_8_), channel_id=1, source_target_pairs={{0,2},{1,3},{2,0},{3,1},{4,6},{5,7},{6,4},{7,5},{8,10},{9,11},{10,... | collective-permute-start | bytes 2555912 | tf_op jit(solution)/shard_map/ppermute | solution.py:1262
  57.3 29.5 %collective-permute-start.7 = (bf16[8,32,1664]{2,1,0:T(8,128)(2,1)S(1)}, bf16[8,32,1664]{2,1,0:T(8,128)(2,1)}, u32[]{:S(2)}, u32[]{:S(2)}) collective-permute-start(bf16[8,32,1664]{2,1,0:T(8,128)(2,1)S(1)} %collective-permute-done.5.refs_3_.refs_11_.refs_9_), channel_id=1, source_target_pairs={{0,2},{1,3},{2,0},{3,1},{4,6},{5,7},{6,4},{7,5},{8,10},{9,11},{10,... | collective-permute-start | bytes 2555912 | tf_op jit(solution)/shard_map/ppermute | solution.py:1262
  75.6 28.6 %collective-permute-start.22 = (bf16[32,3072]{1,0:T(8,128)(2,1)}, bf16[32,3072]{1,0:T(8,128)(2,1)S(1)}, u32[]{:S(2)}, u32[]{:S(2)}) collective-permute-start(bf16[32,3072]{1,0:T(8,128)(2,1)} %copy-done.47), channel_id=1, source_target_pairs={{0,8},{1,9},{2,10},{3,11},{4,12},{5,13},{6,14},{7,15},{8,0},{9,1},... | collective-permute-start | bytes 589832 | tf_op jit(solution)/shard_map/ppermute | solution.py:1262
  84.2 20.0 %collective-permute-start.23 = (bf16[32,3072]{1,0:T(8,128)(2,1)S(1)}, bf16[32,3072]{1,0:T(8,128)(2,1)S(1)}, u32[]{:S(2)}, u32[]{:S(2)}) collective-permute-start(bf16[32,3072]{1,0:T(8,128)(2,1)S(1)} %copy-done.48), channel_id=1, source_target_pairs={{0,16},{1,17},{2,18},{3,19},{4,20},{5,21},{6,22},{7,23},{8,24},{9,... | collective-permute-start | bytes 589832 | tf_op jit(solution)/shard_map/ppermute | solution.py:1262
  85.3 19.0 %collective-permute-start.24 = (bf16[32,3072]{1,0:T(8,128)(2,1)S(1)}, bf16[32,3072]{1,0:T(8,128)(2,1)S(1)}, u32[]{:S(2)}, u32[]{:S(2)}) collective-permute-start(bf16[32,3072]{1,0:T(8,128)(2,1)S(1)} %copy-done.48), channel_id=1, source_target_pairs={{0,24},{1,25},{2,26},{3,27},{4,28},{5,29},{6,30},{7,31},{8,16},{9,... | collective-permute-start | bytes 589832 | tf_op jit(solution)/shard_map/ppermute | solution.py:1262
  113.3 20.8 %collective-permute-start.27 = (bf16[32,4096]{1,0:T(8,128)(2,1)}, bf16[32,4096]{1,0:T(8,128)(2,1)}, u32[]{:S(2)}, u32[]{:S(2)}) collective-permute-start(bf16[32,4096]{1,0:T(8,128)(2,1)} %get-tuple-element.211.refs_0_), channel_id=1, source_target_pairs={{0,8},{1,9},{2,10},{3,11},{4,12},{5,13},{6,14},{7,15},{8,0},{9,1},... | collective-permute-start | bytes 786440 | tf_op jit(solution)/shard_map/ppermute | solution.py:1262
  116.0 21.6 %collective-permute-start.28 = (bf16[32,4096]{1,0:T(8,128)(2,1)}, bf16[32,4096]{1,0:T(8,128)(2,1)S(1)}, u32[]{:S(2)}, u32[]{:S(2)}) collective-permute-start(bf16[32,4096]{1,0:T(8,128)(2,1)} %get-tuple-element.211.refs_0_), channel_id=1, source_target_pairs={{0,16},{1,17},{2,18},{3,19},{4,20},{5,21},{6,22},{7,23},{8,24},{9,... | collective-permute-start | bytes 786440 | tf_op jit(solution)/shard_map/ppermute | solution.py:1262
  117.9 19.7 %collective-permute-start.29 = (bf16[32,4096]{1,0:T(8,128)(2,1)}, bf16[32,4096]{1,0:T(8,128)(2,1)S(1)}, u32[]{:S(2)}, u32[]{:S(2)}) collective-permute-start(bf16[32,4096]{1,0:T(8,128)(2,1)} %get-tuple-element.211.refs_0_), channel_id=1, source_target_pairs={{0,24},{1,25},{2,26},{3,27},{4,28},{5,29},{6,30},{7,31},{8,16},{9,... | collective-permute-start | bytes 786440 | tf_op jit(solution)/shard_map/ppermute | solution.py:1262
  159.7 25.1 %collective-permute-start.38 = (bf16[8,32,2048]{2,1,0:T(8,128)(2,1)}, bf16[8,32,2048]{2,1,0:T(8,128)(2,1)}, u32[]{:S(2)}, u32[]{:S(2)}) collective-permute-start(bf16[8,32,2048]{2,1,0:T(8,128)(2,1)} %get-tuple-element.218.refs_19_.refs_0_), channel_id=1, source_target_pairs={{0,1},{1,0},{2,3},{3,2},{4,5},{5,4},{6,7},{7,6},{8,9},{9,8},{10,11... | collective-permute-start | bytes 3145736 | tf_op jit(solution)/shard_map/ppermute | solution.py:1262
  160.5 24.8 %collective-permute-start.39 = (bf16[8,32,2048]{2,1,0:T(8,128)(2,1)}, bf16[8,32,2048]{2,1,0:T(8,128)(2,1)}, u32[]{:S(2)}, u32[]{:S(2)}) collective-permute-start(bf16[8,32,2048]{2,1,0:T(8,128)(2,1)} %get-tuple-element.219.refs_20_.refs_1_), channel_id=1, source_target_pairs={{0,4},{1,5},{2,6},{3,7},{4,0},{5,1},{6,2},{7,3},{8,12},{9,13},{10,... | collective-permute-start | bytes 3145736 | tf_op jit(solution)/shard_map/ppermute | solution.py:1262
  290.2 19.9 %collective-permute-start.45 = (bf16[8,32,1536]{2,1,0:T(8,128)(2,1)S(1)}, bf16[8,32,1536]{2,1,0:T(8,128)(2,1)S(1)}, u32[]{:S(2)}, u32[]{:S(2)}) collective-permute-start(bf16[8,32,1536]{2,1,0:T(8,128)(2,1)S(1)} %get-tuple-element.255), channel_id=1, source_target_pairs={{0,1},{1,0},{2,3},{3,2},{4,5},{5,4},{6,7},{7,6},{8,9},{9,8},{10,11... | collective-permute-start | bytes 2359304 | tf_op jit(solution)/shard_map/ppermute | solution.py:1262
  290.5 19.6 %collective-permute-start.46 = (bf16[4,64,1536]{2,1,0:T(8,128)(2,1)S(1)}, bf16[4,64,1536]{2,1,0:T(8,128)(2,1)S(1)}, u32[]{:S(2)}, u32[]{:S(2)}) collective-permute-start(bf16[4,64,1536]{2,1,0:T(8,128)(2,1)S(1)} %get-tuple-element.257), channel_id=1, source_target_pairs={{0,4},{1,5},{2,6},{3,7},{4,0},{5,1},{6,2},{7,3},{8,12},{9,13},{10,... | collective-permute-start | bytes 2359304 | tf_op jit(solution)/shard_map/ppermute | solution.py:1262
  326.4 19.5 %collective-permute-start.48 = (bf16[4,32,1536]{2,1,0:T(8,128)(2,1)}, bf16[4,32,1536]{2,1,0:T(8,128)(2,1)}, u32[]{:S(2)}, u32[]{:S(2)}) collective-permute-start(bf16[4,32,1536]{2,1,0:T(8,128)(2,1)} %get-tuple-element.267), channel_id=1, source_target_pairs={{0,4},{1,5},{2,6},{3,7},{4,0},{5,1},{6,2},{7,3},{8,12},{9,13},{10,... | collective-permute-start | bytes 1179656 | tf_op jit(solution)/shard_map/ppermute | solution.py:1262
  344.3 19.7 %collective-permute-start.50 = (bf16[8,32,1536]{2,1,0:T(8,128)(2,1)}, bf16[8,32,1536]{2,1,0:T(8,128)(2,1)}, u32[]{:S(2)}, u32[]{:S(2)}) collective-permute-start(bf16[8,32,1536]{2,1,0:T(8,128)(2,1)} %get-tuple-element.275), channel_id=1, source_target_pairs={{0,1},{1,0},{2,3},{3,2},{4,5},{5,4},{6,7},{7,6},{8,9},{9,8},{10,11... | collective-permute-start | bytes 2359304 | tf_op jit(solution)/shard_map/ppermute | solution.py:1262
  344.7 19.4 %collective-permute-start.51 = (bf16[4,64,1536]{2,1,0:T(8,128)(2,1)}, bf16[4,64,1536]{2,1,0:T(8,128)(2,1)}, u32[]{:S(2)}, u32[]{:S(2)}) collective-permute-start(bf16[4,64,1536]{2,1,0:T(8,128)(2,1)} %get-tuple-element.277), channel_id=1, source_target_pairs={{0,4},{1,5},{2,6},{3,7},{4,0},{5,1},{6,2},{7,3},{8,12},{9,13},{10,... | collective-permute-start | bytes 2359304 | tf_op jit(solution)/shard_map/ppermute | solution.py:1262
  375.7 23.9 %collective-permute-start.54 = (bf16[8,64,3072]{2,1,0:T(8,128)(2,1)}, bf16[8,64,3072]{2,1,0:T(8,128)(2,1)}, u32[]{:S(2)}, u32[]{:S(2)}) collective-permute-start(bf16[8,64,3072]{2,1,0:T(8,128)(2,1)} %get-tuple-element.295), channel_id=1, source_target_pairs={{0,2},{1,3},{2,0},{3,1},{4,6},{5,7},{6,4},{7,5},{8,10},{9,11},{10,... | collective-permute-start | bytes 9437192 | tf_op jit(solution)/shard_map/ppermute | solution.py:1262
  377.2 22.4 %collective-permute-start.56 = (bf16[32,3072]{1,0:T(8,128)(2,1)}, bf16[32,3072]{1,0:T(8,128)(2,1)S(1)}, u32[]{:S(2)}, u32[]{:S(2)}) collective-permute-start(bf16[32,3072]{1,0:T(8,128)(2,1)} %get-tuple-element.297), channel_id=1, source_target_pairs={{0,16},{1,17},{2,18},{3,19},{4,20},{5,21},{6,22},{7,23},{8,24},{9,... | collective-permute-start | bytes 589832 | tf_op jit(solution)/shard_map/ppermute | solution.py:1262
  378.5 21.0 %collective-permute-start.57 = (bf16[32,3072]{1,0:T(8,128)(2,1)}, bf16[32,3072]{1,0:T(8,128)(2,1)S(1)}, u32[]{:S(2)}, u32[]{:S(2)}) collective-permute-start(bf16[32,3072]{1,0:T(8,128)(2,1)} %get-tuple-element.298), channel_id=1, source_target_pairs={{0,24},{1,25},{2,26},{3,27},{4,28},{5,29},{6,30},{7,31},{8,16},{9,... | collective-permute-start | bytes 589832 | tf_op jit(solution)/shard_map/ppermute | solution.py:1262
  386.8 19.3 %collective-permute-start.52 = (bf16[4,32,1536]{2,1,0:T(8,128)(2,1)S(1)}, bf16[4,32,1536]{2,1,0:T(8,128)(2,1)S(1)}, u32[]{:S(2)}, u32[]{:S(2)}) collective-permute-start(bf16[4,32,1536]{2,1,0:T(8,128)(2,1)S(1)} %get-tuple-element.292), channel_id=1, source_target_pairs={{0,4},{1,5},{2,6},{3,7},{4,0},{5,1},{6,2},{7,3},{8,12},{9,13},{10,... | collective-permute-start | bytes 1179656 | tf_op jit(solution)/shard_map/ppermute | solution.py:1262
  450.3 23.2 %collective-permute-start.66 = (bf16[8,32,1280]{2,1,0:T(8,128)(2,1)S(1)}, bf16[8,32,1280]{2,1,0:T(8,128)(2,1)S(1)}, u32[]{:S(2)}, u32[]{:S(2)}) collective-permute-start(bf16[8,32,1280]{2,1,0:T(8,128)(2,1)S(1)} %get-tuple-element.316), channel_id=1, source_target_pairs={{0,1},{1,0},{2,3},{3,2},{4,5},{5,4},{6,7},{7,6},{8,9},{9,8},{10,11... | collective-permute-start | bytes 1966088 | tf_op jit(solution)/shard_map/ppermute | solution.py:1262
  452.0 21.5 %collective-permute-start.67 = (bf16[4,64,1152]{2,1,0:T(8,128)(2,1)S(1)}, bf16[4,64,1152]{2,1,0:T(8,128)(2,1)S(1)}, u32[]{:S(2)}, u32[]{:S(2)}) collective-permute-start(bf16[4,64,1152]{2,1,0:T(8,128)(2,1)S(1)} %get-tuple-element.318), channel_id=1, source_target_pairs={{0,4},{1,5},{2,6},{3,7},{4,0},{5,1},{6,2},{7,3},{8,12},{9,13},{10,... | collective-permute-start | bytes 1769480 | tf_op jit(solution)/shard_map/ppermute | solution.py:1262
  (137 other events, 1232.6 us)
